TPU v7x, 512 devices: a whole 4x8x8 slice. The times are simulated.
512 devices in a mesh: tm: 8 (over x, z_lo), space: 64 (over z_hi, y, core).
Axes of the slice: x: 4, y: 8, z: 8 (z_hi: 4, z_lo: 2; z = z_hi * 2 + z_lo), core: 2. Of those that a mesh axis runs over, the one named last changes fastest.
Arguments:
- model_departure: float32 [8, 1024, 8, 384], P('tm', 'space'), may hold values from -24 to 24, as said below
- obs_departure: float32 [8, 131072], P('tm', 'space'), may hold values from -6 to 6
- obs_variance: float32 [8, 131072], P('tm', 'space'), may hold values from 0.5 to 2
- obs_weight: float32 [8, 8, 131072], P('tm', None, 'space'), may hold values from -2 to 2
- obs_index: int32 [8, 131072], P('tm', 'space'), may hold values from 0 to 6143
- obs_count: int32 [8, 64], P('tm', 'space'), may hold values from 1024 to 2048, as said below
- courant: float32 [8, 1024, 8, 384], P('tm', 'space'), may hold values from 0.3 to 0.95
- diffusion: float32 [8, 8, 384], P('tm'), may hold values from 0.02 to 0.45
- vertical_mix: float32 [8, 8, 8], P('tm'), may hold values from -0.75 to 0.75
- error_variance: float32 [8, 1024, 3072], P('tm', None, 'space'), may hold values from 0.2 to 2
Outputs:
- multiplier: float32 [8, 1024, 8, 384], P('tm', 'space')
- obs_multiplier: float32 [8, 131072], P('tm', 'space')
- increment: float32 [8, 1024, 8, 384], P('tm', 'space')
Inputs may be any that keep to these rules, and one draw needn't show every extreme that they name: `model_departure`: smooth trends and level-latitude scales times random entries; entries lie within -24 to 24. `obs_count`: some tile of some sub-window holds exactly 2048 live slots and some exactly 1024.
All inputs are finite; a program needn't handle non-finite values.
Results may differ from a plain program's by a relative error of at most 0.0001.
Values sent between devices are 32-bit elements; how exact they have to be, the bound alone decides.
A program may use at most 64 MiB of HBM per device.

v0:
```python
import jax
import jax.numpy as jnp
from jax import lax
from jax.sharding import PartitionSpec as P

STEPS = 4
ITERS = 2
HAAR = 6


HALF_ROOT = 0.7071067811865476
PRECISION = lax.Precision.HIGHEST


def extended(value, sides, width):
    for axis, dim in sides:
        peers, length = (lax.axis_size(axis), value.shape[dim])
        up = [(i, (i + 1) % peers) for i in range(peers)]
        down = [(j, i) for i, j in up]
        last = lax.slice_in_dim(value, length - width, length, axis=dim)
        initial = lax.slice_in_dim(value, 0, width, axis=dim)
        before = lax.ppermute(last, axis, up)
        after = lax.ppermute(initial, axis, down)
        value = jnp.concatenate([before, value, after], axis=dim)
    return value


def passed_along(value, axis, by):
    peers = lax.axis_size(axis)
    pairs = [(i, i + by) for i in range(peers) if 0 <= i + by < peers]
    return lax.ppermute(value, axis, pairs)


def wavelet_forward(values, first_level, last_level):
    length, columns = values.shape
    for level_index in range(first_level, last_level + 1):
        block_size = 2**level_index
        shaped = values.reshape(length // block_size, 2, block_size // 2, columns)
        lower_part = shaped[:, 0, 0]
        upper_part = shaped[:, 1, 0]
        shaped = shaped.at[:, 0, 0].set((lower_part + upper_part) * HALF_ROOT)
        shaped = shaped.at[:, 1, 0].set((lower_part - upper_part) * HALF_ROOT)
        values = shaped.reshape(length, columns)
    return values


def wavelet_inverse(values, first_level, last_level):
    length, columns = values.shape
    for level_index in range(last_level, first_level - 1, -1):
        block_size = 2**level_index
        shaped = values.reshape(length // block_size, 2, block_size // 2, columns)
        coarse = shaped[:, 0, 0]
        detail = shaped[:, 1, 0]
        shaped = shaped.at[:, 0, 0].set((coarse + detail) * HALF_ROOT)
        shaped = shaped.at[:, 1, 0].set((coarse - detail) * HALF_ROOT)
        values = shaped.reshape(length, columns)
    return values


def advection_weights(courant):
    squared = courant * courant
    return ((squared + courant) * 0.5, 1.0 - squared, (squared - courant) * 0.5)


def meridional(values, diffusion):
    fluxes = diffusion[:, :-1] * (values[..., 1:] - values[..., :-1])
    border = jnp.zeros_like(values[..., :1])
    return (
        values
        + jnp.concatenate([fluxes, border], axis=-1)
        - jnp.concatenate([border, fluxes], axis=-1)
    )


def vertical(values, mixing):
    return jnp.einsum("lm,nmj->nlj", mixing, values, precision=PRECISION)


def vertical_adjoint(values, mixing):
    return jnp.einsum("ml,nmj->nlj", mixing, values, precision=PRECISION)


def propagate(forward_in, backward_in, courant, diffusion, mixing):
    west_weight, centre_weight, east_weight = advection_weights(courant)
    forward_state = forward_in
    backward_state = backward_in
    for step_index in range(STEPS):
        spread_out = meridional(vertical_adjoint(backward_state, mixing), diffusion)
        west_terms = west_weight * spread_out
        east_terms = east_weight * spread_out
        edge_cells = jnp.stack(
            [
                jnp.concatenate([forward_state[:1], forward_state[-1:]]),
                jnp.concatenate([west_terms[:1], east_terms[-1:]]),
            ]
        )
        rim_cells = extended(edge_cells, (("space", 1),), 1)
        behind = rim_cells[:, 0]
        beyond = rim_cells[:, 3]
        previous = jnp.concatenate([behind[0][None], forward_state[:-1]])
        following = jnp.concatenate([forward_state[1:], beyond[0][None]])
        advected = west_weight * previous + centre_weight * forward_state + east_weight * following
        forward_state = vertical(meridional(advected, diffusion), mixing)
        backward_state = (
            centre_weight * spread_out
            + jnp.concatenate([west_terms[1:], beyond[1][None]])
            + jnp.concatenate([behind[1][None], east_terms[:-1]])
        )
    return (forward_state, backward_state)


def covary(state, variance_columns):
    local_lon, levels, lat_rows = state.shape
    flattened = state.reshape(1, local_lon, levels * lat_rows)
    columns = lax.all_to_all(flattened, "space", split_axis=2, concat_axis=1, tiled=True)
    scaled = wavelet_inverse(wavelet_forward(columns[0], 1, HAAR) * variance_columns, 1, HAAR)
    result = lax.all_to_all(scaled[None], "space", split_axis=1, concat_axis=2, tiled=True)[0]
    return result.reshape(local_lon, levels, lat_rows)


def body(
    model_departure,
    obs_departure,
    obs_variance,
    obs_weight,
    obs_index,
    obs_count,
    courant,
    diffusion,
    vertical_mix,
    error_variance,
):
    lat_rows = courant.shape[3]
    levels = courant.shape[2]
    mixing = 0.7 * jnp.eye(levels, dtype=jnp.float32) + vertical_mix[0]
    own_courant = courant[0]
    own_diffusion = diffusion[0]
    own_weight = obs_weight[0]
    slot_count = obs_index.shape[1]
    live_slots = (jnp.arange(slot_count, dtype=jnp.int32) < obs_count[0, 0]).astype(jnp.float32)
    lon_index = obs_index[0] // lat_rows
    lat_index = obs_index[0] % lat_rows
    variance_columns = error_variance[0]
    multiplier = jnp.zeros_like(own_courant)
    obs_multiplier = jnp.zeros_like(obs_departure[0])
    increment = jnp.zeros_like(own_courant)
    res_lam = model_departure[0]
    res_obs = live_slots * obs_departure[0]
    res_state = jnp.zeros_like(own_courant)
    for iter_index in range(ITERS):
        later_rx = passed_along(res_state, "tm", -1)
        covaried = covary(res_state, variance_columns)
        search_lam = res_state
        search_obs = res_obs / obs_variance[0]
        search_state = res_lam - covaried
        forward_out, backward_out = propagate(
            search_state, later_rx, own_courant, own_diffusion, mixing
        )
        earlier = passed_along(forward_out, "tm", 1)
        image_lam = covaried + (search_state - earlier)
        picked = search_state[lon_index, :, lat_index]
        image_obs = (
            res_obs + jnp.einsum("ol,lo->o", picked, own_weight, precision=PRECISION) * live_slots
        )
        terms = jnp.swapaxes(own_weight * search_obs[None, :], 0, 1)
        image_state = (
            search_lam
            - backward_out
            + jnp.zeros_like(own_courant).at[lon_index, :, lat_index].add(terms)
        )
        numerator = (
            jnp.sum(res_lam * image_lam)
            + jnp.sum(res_obs * image_obs)
            + jnp.sum(res_state * image_state)
        )
        denominator = (
            jnp.sum(image_lam * image_lam)
            + jnp.sum(image_obs * image_obs)
            + jnp.sum(image_state * image_state)
        )
        numerator, denominator = lax.psum((numerator, denominator), ("tm", "space"))
        step_size = numerator / (denominator + 1e-06)
        multiplier = multiplier + step_size * search_lam
        obs_multiplier = obs_multiplier + step_size * search_obs
        increment = increment + step_size * search_state
        res_lam = res_lam - step_size * image_lam
        res_obs = res_obs - step_size * image_obs
        res_state = res_state - step_size * image_state
    return (multiplier[None], obs_multiplier[None], increment[None])


def solution(mesh):
    in_specs = (
        P("tm", "space", None, None),
        P("tm", "space"),
        P("tm", "space"),
        P("tm", None, "space"),
        P("tm", "space"),
        P("tm", "space"),
        P("tm", "space", None, None),
        P("tm", None, None),
        P("tm", None, None),
        P("tm", None, "space"),
    )
    out_specs = (P("tm", "space", None, None), P("tm", "space"), P("tm", "space", None, None))
    return jax.shard_map(body, mesh=mesh, in_specs=in_specs, out_specs=out_specs, check_vma=False)
```

profile of v0, /device:TPU:1, one launch (start us, length us, event | category | flops | bytes accessed | tf_op | source)
XLA Modules:
  0.0 573.7 jit_solution(13404665758945877612)
XLA Ops:
  12.9 17.6 %all-to-all-start = ((f32[64,1,768]{2,1,0:T(1,128)}), f32[64,1,768]{2,1,0:T(1,128)S(1)}, u32[]{:S(2)}, u32[]{:S(2)}) async-start(f32[64,1,768]{2,1,0:T(1,128)} %reshape.1794), calls=%async_computation | async-start | bytes 393216 | tf_op jit(solution)/shard_map/all_to_all | solution.py:117
  37.5 6.4 %all-to-all-done = f32[64,1,768]{2,1,0:T(1,128)S(1)} async-done(((f32[64,1,768]{2,1,0:T(1,128)}), f32[64,1,768]{2,1,0:T(1,128)S(1)}, u32[]{:S(2)}, u32[]{:S(2)}) %all-to-all-start) | async-done | bytes 196640 | tf_op jit(solution)/shard_map/all_to_all | solution.py:117
  55.8 22.6 %gather_fusion = f32[2048,8]{1,0:T(8,128)} fusion(f32[16,8,384]{1,2,0:T(8,128)S(1)} %copy.153, s32[2048]{0:T(1024)S(1)} %bitcast.456), kind=kCustom, calls=%fused_computation | custom fusion | bytes 147456 | tf_op jit(solution)/shard_map/gather | solution.py:161
  90.7 4.8 collective-permute-start.4
  99.7 8.5 %collective-permute-start.6 = (f32[2,1,8,384]{3,2,1,0:T(8,128)S(1)}, f32[2,1,8,384]{3,2,1,0:T(8,128)S(1)}, u32[]{:S(2)}, u32[]{:S(2)}) collective-permute-start(f32[2,1,8,384]{3,2,1,0:T(8,128)S(1)} %get-tuple-element.704), channel_id=1, source_target_pairs={{1,0},{2,1},{3,2},{4,3},{5,4},{6,5},{7,6},{8,7},{9,8},{10,9},{11,1... | collective-permute-start | bytes 73736 | tf_op jit(solution)/shard_map/ppermute | solution.py:23
  112.3 8.5 %collective-permute-start.8 = (f32[2,1,8,384]{3,2,1,0:T(8,128)S(1)}, f32[2,1,8,384]{3,2,1,0:T(8,128)S(1)}, u32[]{:S(2)}, u32[]{:S(2)}) collective-permute-start(f32[2,1,8,384]{3,2,1,0:T(8,128)S(1)} %get-tuple-element.702), channel_id=1, source_target_pairs={{1,0},{2,1},{3,2},{4,3},{5,4},{6,5},{7,6},{8,7},{9,8},{10,9},{11,1... | collective-permute-start | bytes 73736 | tf_op jit(solution)/shard_map/ppermute | solution.py:23
  123.7 5.0 collective-permute-start.9
  130.6 13.0 %scatter_fusion = f32[6144,8]{1,0:T(8,128)S(1)} fusion(f32[6144,8]{1,0:T(8,128)S(1)} %copy.154, s32[2048]{0:T(1024)} %broadcast_select_fusion, f32[2048,8]{1,0:T(8,128)} %copy.155), kind=kCustom, calls=%fused_computation.2 | custom fusion | flops 16384 | bytes 204800
  154.4 105.4 %all-reduce.33 = (f32[]{:T(128)}, f32[]{:T(128)}) all-reduce(f32[]{:T(128)S(6)} %add.541, f32[]{:T(128)S(6)} %add.543), channel_id=1, replica_groups=mesh['tm'=8,'space'=64] {'tm','space'}, use_global_device_ids=true, to_apply=%region_4.5 | all-reduce | flops 2 | bytes 16 | tf_op jit(solution)/shard_map/psum | solution.py:181
  265.5 13.7 %reduce.112 = f32[3072,16]{1,0:T(8,128)S(1)} reduce(f32[3072,1,16]{2,1,0:T(1,128)S(1)} %bitcast.465, f32[]{:T(128)} %broadcast.1117), dimensions={1}, to_apply=%bitcast.440.reduce_sub_computation | reduce | bytes 393220
  280.4 7.3 %all-to-all-start.1 = ((f32[64,1,768]{2,1,0:T(1,128)}), f32[64,1,768]{2,1,0:T(1,128)S(1)}, u32[]{:S(2)}, u32[]{:S(2)}) async-start(f32[64,1,768]{2,1,0:T(1,128)} %reshape.1796), calls=%async_computation.1 | async-start | bytes 393216 | tf_op jit(solution)/shard_map/all_to_all | solution.py:115
  292.5 8.3 %all-to-all-done.1 = f32[64,1,768]{2,1,0:T(1,128)S(1)} async-done(((f32[64,1,768]{2,1,0:T(1,128)}), f32[64,1,768]{2,1,0:T(1,128)S(1)}, u32[]{:S(2)}, u32[]{:S(2)}) %all-to-all-start.1) | async-done | bytes 196640 | tf_op jit(solution)/shard_map/all_to_all | solution.py:115
  306.3 6.0 %scatter.145 = f32[512,2,1,48]{3,1,0,2:T(2,128)S(1)} dynamic-update-slice(f32[512,2,1,48]{3,1,0,2:T(2,128)S(1)} %bitcast.469, f32[512,1,1,48]{3,1,0,2:T(1,128)S(1)} %bitcast.520, s32[]{:T(128)} %constant.1192.clone.1, s32[]{:T(128)} %constant.1192.clone.1, s32[]{:T(128)} %constant.1192.clone.1, s32[]{:T(128)} %constant.1192.clone.1) | dynamic-update-slice | bytes 196612 | tf_op jit(solution)/shard_map/scatter | solution.py:41
  312.3 6.0 %scatter.146 = f32[512,2,1,48]{3,1,0,2:T(2,128)S(1)} dynamic-update-slice(f32[512,2,1,48]{3,1,0,2:T(2,128)S(1)} %scatter.145, f32[512,1,1,48]{3,1,0,2:T(1,128)S(1)} %bitcast.519, s32[]{:T(128)} %constant.1192.clone.1, s32[]{:T(128)} %constant.1193.clone.1, s32[]{:T(128)} %constant.1192.clone.1, s32[]{:T(128)} %constant.1192.clone.1) | dynamic-update-slice | bytes 196612 | tf_op jit(solution)/shard_map/scatter | solution.py:42
  338.8 5.2 all-to-all-start.2
  346.3 11.1 %all-to-all-done.2 = f32[64,1,768]{2,1,0:T(1,128)S(1)} async-done(((f32[64,1,768]{2,1,0:T(1,128)}), f32[64,1,768]{2,1,0:T(1,128)S(1)}, u32[]{:S(2)}, u32[]{:S(2)}) %all-to-all-start.2) | async-done | bytes 196640 | tf_op jit(solution)/shard_map/all_to_all | solution.py:117
  371.0 22.6 %gather_fusion.1 = f32[2048,8]{1,0:T(8,128)} fusion(f32[16,8,384]{1,2,0:T(8,128)S(1)} %copy.189, s32[2048]{0:T(1024)S(1)} %bitcast.457), kind=kCustom, calls=%fused_computation.1 | custom fusion | bytes 147456 | tf_op jit(solution)/shard_map/gather | solution.py:161
  402.8 3.6 collective-permute-start.13
  406.5 4.1 collective-permute-done.13
  411.8 8.9 %collective-permute-start.16 = (f32[2,1,8,384]{3,2,1,0:T(8,128)S(1)}, f32[2,1,8,384]{3,2,1,0:T(8,128)S(1)}, u32[]{:S(2)}, u32[]{:S(2)}) collective-permute-start(f32[2,1,8,384]{3,2,1,0:T(8,128)S(1)} %get-tuple-element.691), channel_id=1, source_target_pairs={{1,0},{2,1},{3,2},{4,3},{5,4},{6,5},{7,6},{8,7},{9,8},{10,9},{11,1... | collective-permute-start | bytes 73736 | tf_op jit(solution)/shard_map/ppermute | solution.py:23
  425.2 8.2 %collective-permute-start.18 = (f32[2,1,8,384]{3,2,1,0:T(8,128)S(1)}, f32[2,1,8,384]{3,2,1,0:T(8,128)S(1)}, u32[]{:S(2)}, u32[]{:S(2)}) collective-permute-start(f32[2,1,8,384]{3,2,1,0:T(8,128)S(1)} %get-tuple-element.689), channel_id=1, source_target_pairs={{1,0},{2,1},{3,2},{4,3},{5,4},{6,5},{7,6},{8,7},{9,8},{10,9},{11,1... | collective-permute-start | bytes 73736 | tf_op jit(solution)/shard_map/ppermute | solution.py:23
  439.6 4.7 collective-permute-start.19
  446.7 13.0 %scatter_fusion.1 = f32[6144,8]{1,0:T(8,128)S(1)} fusion(f32[6144,8]{1,0:T(8,128)S(1)} %copy.190, s32[2048]{0:T(1024)} %broadcast_select_fusion, f32[2048,8]{1,0:T(8,128)} %copy.191), kind=kCustom, calls=%fused_computation.3 | custom fusion | flops 16384 | bytes 204800
  468.6 99.9 %all-reduce.32 = (f32[]{:T(128)}, f32[]{:T(128)}) all-reduce(f32[]{:T(128)S(6)} %add.584, f32[]{:T(128)S(6)} %add.586), channel_id=1, replica_groups=mesh['tm'=8,'space'=64] {'tm','space'}, use_global_device_ids=true, to_apply=%region_13.14 | all-reduce | flops 2 | bytes 16 | tf_op jit(solution)/shard_map/psum | solution.py:181
  (372 shorter events, 145.7 us)
Async XLA Ops:
  0.7 32.9 %collective-permute-start = (f32[16,8,384]{2,1,0:T(8,128)S(1)}, f32[16,8,384]{2,1,0:T(8,128)S(1)}, u32[]{:S(2)}, u32[]{:S(2)}) collective-permute-start(f32[16,8,384]{2,1,0:T(8,128)S(1)} %broadcast.837), channel_id=1, source_target_pairs={{64,0},{128,64},{192,128},{256,192},{320,256},{384,320},{448,384},... | collective-permute-start | bytes 589832 | tf_op jit(solution)/shard_map/ppermute | solution.py:31
  12.9 31.0 %all-to-all-start = ((f32[64,1,768]{2,1,0:T(1,128)}), f32[64,1,768]{2,1,0:T(1,128)S(1)}, u32[]{:S(2)}, u32[]{:S(2)}) async-start(f32[64,1,768]{2,1,0:T(1,128)} %reshape.1794), calls=%async_computation | async-start | bytes 393216 | tf_op jit(solution)/shard_map/all_to_all | solution.py:117
  50.3 31.9 %collective-permute-start.1 = (f32[2,1,8,384]{3,2,1,0:T(8,128)}, f32[2,1,8,384]{3,2,1,0:T(8,128)}, u32[]{:S(2)}, u32[]{:S(2)}) collective-permute-start(f32[2,1,8,384]{3,2,1,0:T(8,128)} %get-tuple-element.707), channel_id=1, source_target_pairs={{0,1},{1,2},{2,3},{3,4},{4,5},{5,6},{6,7},{7,8},{8,9},{9,10},{10,1... | collective-permute-start | bytes 73736 | tf_op jit(solution)/shard_map/ppermute | solution.py:22
  53.7 29.3 %collective-permute-start.2 = (f32[2,1,8,384]{3,2,1,0:T(8,128)}, f32[2,1,8,384]{3,2,1,0:T(8,128)}, u32[]{:S(2)}, u32[]{:S(2)}) collective-permute-start(f32[2,1,8,384]{3,2,1,0:T(8,128)} %get-tuple-element.708), channel_id=1, source_target_pairs={{1,0},{2,1},{3,2},{4,3},{5,4},{6,5},{7,6},{8,7},{9,8},{10,9},{11,1... | collective-permute-start | bytes 73736 | tf_op jit(solution)/shard_map/ppermute | solution.py:23
  87.0 8.6 %collective-permute-start.3 = (f32[2,1,8,384]{3,2,1,0:T(8,128)S(1)}, f32[2,1,8,384]{3,2,1,0:T(8,128)S(1)}, u32[]{:S(2)}, u32[]{:S(2)}) collective-permute-start(f32[2,1,8,384]{3,2,1,0:T(8,128)S(1)} %get-tuple-element.705), channel_id=1, source_target_pairs={{0,1},{1,2},{2,3},{3,4},{4,5},{5,6},{6,7},{7,8},{8,9},{9,10},{10,1... | collective-permute-start | bytes 73736 | tf_op jit(solution)/shard_map/ppermute | solution.py:22
  90.7 5.7 collective-permute-start.4
  97.7 10.5 %collective-permute-start.5 = (f32[2,1,8,384]{3,2,1,0:T(8,128)S(1)}, f32[2,1,8,384]{3,2,1,0:T(8,128)S(1)}, u32[]{:S(2)}, u32[]{:S(2)}) collective-permute-start(f32[2,1,8,384]{3,2,1,0:T(8,128)S(1)} %get-tuple-element.703), channel_id=1, source_target_pairs={{0,1},{1,2},{2,3},{3,4},{4,5},{5,6},{6,7},{7,8},{8,9},{9,10},{10,1... | collective-permute-start | bytes 73736 | tf_op jit(solution)/shard_map/ppermute | solution.py:22
  99.7 9.4 %collective-permute-start.6 = (f32[2,1,8,384]{3,2,1,0:T(8,128)S(1)}, f32[2,1,8,384]{3,2,1,0:T(8,128)S(1)}, u32[]{:S(2)}, u32[]{:S(2)}) collective-permute-start(f32[2,1,8,384]{3,2,1,0:T(8,128)S(1)} %get-tuple-element.704), channel_id=1, source_target_pairs={{1,0},{2,1},{3,2},{4,3},{5,4},{6,5},{7,6},{8,7},{9,8},{10,9},{11,1... | collective-permute-start | bytes 73736 | tf_op jit(solution)/shard_map/ppermute | solution.py:23
  110.3 10.5 %collective-permute-start.7 = (f32[2,1,8,384]{3,2,1,0:T(8,128)S(1)}, f32[2,1,8,384]{3,2,1,0:T(8,128)S(1)}, u32[]{:S(2)}, u32[]{:S(2)}) collective-permute-start(f32[2,1,8,384]{3,2,1,0:T(8,128)S(1)} %get-tuple-element.701), channel_id=1, source_target_pairs={{0,1},{1,2},{2,3},{3,4},{4,5},{5,6},{6,7},{7,8},{8,9},{9,10},{10,1... | collective-permute-start | bytes 73736 | tf_op jit(solution)/shard_map/ppermute | solution.py:22
  112.3 9.4 %collective-permute-start.8 = (f32[2,1,8,384]{3,2,1,0:T(8,128)S(1)}, f32[2,1,8,384]{3,2,1,0:T(8,128)S(1)}, u32[]{:S(2)}, u32[]{:S(2)}) collective-permute-start(f32[2,1,8,384]{3,2,1,0:T(8,128)S(1)} %get-tuple-element.702), channel_id=1, source_target_pairs={{1,0},{2,1},{3,2},{4,3},{5,4},{6,5},{7,6},{8,7},{9,8},{10,9},{11,1... | collective-permute-start | bytes 73736 | tf_op jit(solution)/shard_map/ppermute | solution.py:23
  123.7 24.7 %collective-permute-start.9 = (f32[16,8,384]{2,1,0:T(8,128)}, f32[16,8,384]{2,1,0:T(8,128)}, u32[]{:S(2)}, u32[]{:S(2)}) collective-permute-start(f32[16,8,384]{2,1,0:T(8,128)} %convolution_bitcast_fusion.8), channel_id=1, source_target_pairs={{0,64},{64,128},{128,192},{192,256},{256,320},{320,384},{384,448},... | collective-permute-start | bytes 589832 | tf_op jit(solution)/shard_map/ppermute | solution.py:31
  262.8 28.5 %collective-permute-start.10 = (f32[16,8,384]{2,1,0:T(8,128)}, f32[16,8,384]{2,1,0:T(8,128)}, u32[]{:S(2)}, u32[]{:S(2)}) collective-permute-start(f32[16,8,384]{2,1,0:T(8,128)} %bitcast.66), channel_id=1, source_target_pairs={{64,0},{128,64},{192,128},{256,192},{320,256},{384,320},{448,384},... | collective-permute-start | bytes 589832 | tf_op jit(solution)/shard_map/ppermute | solution.py:31
  280.4 20.5 %all-to-all-start.1 = ((f32[64,1,768]{2,1,0:T(1,128)}), f32[64,1,768]{2,1,0:T(1,128)S(1)}, u32[]{:S(2)}, u32[]{:S(2)}) async-start(f32[64,1,768]{2,1,0:T(1,128)} %reshape.1796), calls=%async_computation.1 | async-start | bytes 393216 | tf_op jit(solution)/shard_map/all_to_all | solution.py:115
  338.8 18.5 %all-to-all-start.2 = ((f32[64,1,768]{2,1,0:T(1,128)}), f32[64,1,768]{2,1,0:T(1,128)S(1)}, u32[]{:S(2)}, u32[]{:S(2)}) async-start(f32[64,1,768]{2,1,0:T(1,128)} %reshape.1798), calls=%async_computation.2 | async-start | bytes 393216 | tf_op jit(solution)/shard_map/all_to_all | solution.py:117
  365.4 30.7 %collective-permute-start.12 = (f32[2,1,8,384]{3,2,1,0:T(8,128)}, f32[2,1,8,384]{3,2,1,0:T(8,128)}, u32[]{:S(2)}, u32[]{:S(2)}) collective-permute-start(f32[2,1,8,384]{3,2,1,0:T(8,128)} %get-tuple-element.695), channel_id=1, source_target_pairs={{1,0},{2,1},{3,2},{4,3},{5,4},{6,5},{7,6},{8,7},{9,8},{10,9},{11,1... | collective-permute-start | bytes 73736 | tf_op jit(solution)/shard_map/ppermute | solution.py:23
  367.4 29.3 %collective-permute-start.11 = (f32[2,1,8,384]{3,2,1,0:T(8,128)}, f32[2,1,8,384]{3,2,1,0:T(8,128)}, u32[]{:S(2)}, u32[]{:S(2)}) collective-permute-start(f32[2,1,8,384]{3,2,1,0:T(8,128)} %get-tuple-element.696), channel_id=1, source_target_pairs={{0,1},{1,2},{2,3},{3,4},{4,5},{5,6},{6,7},{7,8},{8,9},{9,10},{10,1... | collective-permute-start | bytes 73736 | tf_op jit(solution)/shard_map/ppermute | solution.py:22
  400.8 5.7 collective-permute-start.14
  402.8 7.7 %collective-permute-start.13 = (f32[2,1,8,384]{3,2,1,0:T(8,128)S(1)}, f32[2,1,8,384]{3,2,1,0:T(8,128)S(1)}, u32[]{:S(2)}, u32[]{:S(2)}) collective-permute-start(f32[2,1,8,384]{3,2,1,0:T(8,128)S(1)} %get-tuple-element.694), channel_id=1, source_target_pairs={{0,1},{1,2},{2,3},{3,4},{4,5},{5,6},{6,7},{7,8},{8,9},{9,10},{10,1... | collective-permute-start | bytes 73736 | tf_op jit(solution)/shard_map/ppermute | solution.py:22
  411.8 11.2 %collective-permute-start.16 = (f32[2,1,8,384]{3,2,1,0:T(8,128)S(1)}, f32[2,1,8,384]{3,2,1,0:T(8,128)S(1)}, u32[]{:S(2)}, u32[]{:S(2)}) collective-permute-start(f32[2,1,8,384]{3,2,1,0:T(8,128)S(1)} %get-tuple-element.691), channel_id=1, source_target_pairs={{1,0},{2,1},{3,2},{4,3},{5,4},{6,5},{7,6},{8,7},{9,8},{10,9},{11,1... | collective-permute-start | bytes 73736 | tf_op jit(solution)/shard_map/ppermute | solution.py:23
  420.9 3.1 collective-permute-start.15
  425.2 10.2 %collective-permute-start.18 = (f32[2,1,8,384]{3,2,1,0:T(8,128)S(1)}, f32[2,1,8,384]{3,2,1,0:T(8,128)S(1)}, u32[]{:S(2)}, u32[]{:S(2)}) collective-permute-start(f32[2,1,8,384]{3,2,1,0:T(8,128)S(1)} %get-tuple-element.689), channel_id=1, source_target_pairs={{1,0},{2,1},{3,2},{4,3},{5,4},{6,5},{7,6},{8,7},{9,8},{10,9},{11,1... | collective-permute-start | bytes 73736 | tf_op jit(solution)/shard_map/ppermute | solution.py:23
  433.5 3.1 collective-permute-start.17
  439.6 23.6 %collective-permute-start.19 = (f32[16,8,384]{2,1,0:T(8,128)}, f32[16,8,384]{2,1,0:T(8,128)}, u32[]{:S(2)}, u32[]{:S(2)}) collective-permute-start(f32[16,8,384]{2,1,0:T(8,128)} %convolution_bitcast_fusion), channel_id=1, source_target_pairs={{0,64},{64,128},{128,192},{192,256},{256,320},{320,384},{384,448},... | collective-permute-start | bytes 589832 | tf_op jit(solution)/shard_map/ppermute | solution.py:31
  446.7 123.8 %copy-start.28 = (f32[1,2048]{1,0:T(1,128)S(1)}, f32[1,2048]{1,0:T(1,128)}, u32[]{:S(2)}) copy-start(f32[1,2048]{1,0:T(1,128)} %param.107) | copy-start | bytes 24580
  (36 other events, 615.9 us)
where the time goes:
time: 584 us; the launch traced here: 574 us
  blocking collectives  205 us (35%)
  local copies, waits for them, and re-layouts  120 us (21%)
  starting transfers between devices  109 us (19%)
  other arithmetic  80.2 us (14%)
  waiting for transfers between devices  34.4 us (6%)
  between operations  13.6 us (2%)
  matrix products  11.1 us (2%)
    psum x2, blocking collectives, body(): numerator, denominator = lax.psum((numerator, denominator), ('tm', 'space'))  205 us
    gather x2, local copies, waits for them, and re-layouts, body(): picked = search_state[lon_index, :, lat_index]  45.2 us
    ppermute x8, starting transfers between devices, extended(): after = lax.ppermute(initial, axis, down)  45.1 us
    unnamed x8, other arithmetic  44.4 us
    all_to_all x2, starting transfers between devices, covary(): lax.all_to_all(scaled[None], 'space', split_axis=1, concat_axis=2, tiled=...  22.8 us
    unnamed x98, local copies, waits for them, and re-layouts  22.1 us
    ppermute x8, starting transfers between devices, extended(): before = lax.ppermute(last, axis, up)  22.1 us
    all_to_all x2, waiting for transfers between devices, covary(): lax.all_to_all(scaled[None], 'space', split_axis=1, concat_axis=2, tiled=...  17.5 us
  transfers between devices with their start and end apart: 23, of which 9 were waited for; matrix products, arithmetic and copies ran while one was open for 23% of the time, Pallas kernels for 0%

commit v1 on v0

v1 whole, which is shorter than its diff:
```python
import jax
import jax.numpy as jnp
from jax import lax
from jax.experimental import pallas as pl
from jax.experimental.pallas import tpu as pltpu
from jax.sharding import PartitionSpec as P

MESH = pl.DeviceIdType.MESH
F32 = jnp.float32
BF16 = jnp.bfloat16
LON, LEV, LAT, SLOTS = 16, 8, 384, 2048
WINDOWS, TILES, SIDE = 8, 64, 8
HALO = 4
WIDE = LON + 2 * HALO + 2
CHUNK = 512
COLUMNS = TILES * LON * LEV * LAT // (TILES * TILES * LON)


def kernel(
    md, od, ov, ow, oi, oc, cr, df, vm, ev,
    mult, omult, incr,
    ac, wts, onehot, lonb, obs, oiv, wv, dfv, vmv, latc, mixf, mixb,
    gb, gx, bufa, bufb, bufg, mo, ma, mdd, mtg, htq, bb, cb, dx,
    hb, cu, r1, s2, r2, vb, al, arr,
    sem_load, sem_hs, sem_hr, sem_1s, sem_1r, sem_2s, sem_2r, sem_cs, sem_cr, sem_gs, sem_gr, sem_ts, sem_tr, sem_as, sem_ar,
):
    k = lax.axis_index("tm")
    t = lax.axis_index("space")
    p, q = t // SIDE, t % SIDE
    east, west = (t + 1) % TILES, (t + TILES - 1) % TILES
    later, before = (k + 1) % WINDOWS, (k + WINDOWS - 1) % WINDOWS

    def send(src, dst, ssem, rsem, kk, tt):
        return pltpu.make_async_remote_copy(
            src_ref=src, dst_ref=dst, send_sem=ssem, recv_sem=rsem, device_id=(kk, tt), device_id_type=MESH
        )

    loads = [
        pltpu.make_async_copy(src, dst, sem_load.at[n])
        for n, (src, dst) in enumerate(
            [
                (md, ac.at[0, pl.ds(HALO, LON)]),
                (cr, ac.at[1, pl.ds(HALO, LON)]),
                (oi, oiv),
                (od, obs.at[0]),
                (ov, obs.at[1]),
                (ow, wv),
                (df, dfv),
                (vm, vmv),
            ]
        )
    ]
    for load in loads:
        load.start()

    barrier = pltpu.get_barrier_semaphore()

    def greet(kk, tt):
        pl.semaphore_signal(barrier, inc=1, device_id=(kk, tt), device_id_type=MESH)

    greet(k, east)
    greet(k, west)
    greet(later, east)
    greet(later, west)
    for j in range(1, SIDE):
        greet(k, p * SIDE + (q + j) % SIDE)
        greet(k, ((p + j) % SIDE) * SIDE + q)
        greet((k + j) % WINDOWS, t)
    for lev in range(LEV):

        @pl.when(lev * SIDE + p != t)
        def _():
            greet(k, lev * SIDE + p)

    for load in loads:
        load.wait()

    index = oiv[...]
    lon = (index * 10923) >> 22
    lat = index - lon * LAT
    lonb[...] = jnp.broadcast_to(lon, (LEV, SLOTS))
    for c in range(SLOTS // CHUNK):
        cols = pl.ds(c * CHUNK, CHUNK)
        rows = lax.broadcasted_iota(jnp.int32, (LAT, CHUNK), 0)
        onehot[:, cols] = jnp.where(rows == lat[:, c * CHUNK : (c + 1) * CHUNK], 1.0, 0.0).astype(BF16)
    live = lax.broadcasted_iota(jnp.int32, (1, SLOTS), 1) < oc[0, 0]
    o0 = jnp.where(live, obs[0], 0.0)
    s1 = o0 / obs[1]
    obs[0] = o0
    obs[2] = s1

    def pieces(x):
        high = x.astype(BF16)
        return high, (x - high.astype(F32)).astype(BF16)

    def spread(row, out):
        total = jnp.zeros((LON * LEV, LAT), F32)
        for c in range(SLOTS // CHUNK):
            cols = pl.ds(c * CHUNK, CHUNK)
            terms = wv[:, cols] * obs[row, :, cols]
            ids = lax.broadcasted_iota(jnp.int32, (LON, LEV, CHUNK), 0)
            placed = jnp.where(ids == lonb[:, cols][None], terms[None], 0.0).reshape(LON * LEV, CHUNK)
            for piece in pieces(placed):
                total += lax.dot_general(piece, onehot[:, cols], (((1,), (1,)), ((), ())), preferred_element_type=F32)
        out[...] = total.reshape(LON, LEV, LAT)

    def observe(field, row):
        high, low = pieces(field.reshape(LON * LEV, LAT))
        for c in range(SLOTS // CHUNK):
            cols = pl.ds(c * CHUNK, CHUNK)
            picked = jnp.dot(high, onehot[:, cols], preferred_element_type=F32)
            picked += jnp.dot(low, onehot[:, cols], preferred_element_type=F32)
            picked = picked.reshape(LON, LEV, CHUNK)
            here = lonb[:, cols]
            column = jnp.zeros((LEV, CHUNK), F32)
            for i in range(LON):
                column = jnp.where(here == i, picked[i], column)
            total = jnp.sum(column * wv[:, cols], axis=0, keepdims=True)
            slot = lax.broadcasted_iota(jnp.int32, (1, CHUNK), 1) + c * CHUNK
            obs[row, :, cols] = jnp.where(slot < oc[0, 0], total, 0.0)

    pl.semaphore_wait(barrier, 32 + jnp.where(p == q, 0, 1))

    halo = [
        send(ac.at[:, pl.ds(HALO, HALO)], ac.at[:, pl.ds(HALO + LON, HALO)], sem_hs.at[0], sem_hr.at[0], k, west),
        send(ac.at[:, pl.ds(LON, HALO)], ac.at[:, pl.ds(0, HALO)], sem_hs.at[1], sem_hr.at[1], k, east),
    ]
    for copy in halo:
        copy.start()

    first = []
    for j in range(1, SIDE):
        peer = (q + j) % SIDE
        back = (q + SIDE - j) % SIDE
        out = send(
            ev.at[:, pl.ds(pl.multiple_of(peer * 128, 128), 128)], r1.at[q], sem_1s.at[j], sem_1r.at[j], k, p * SIDE + peer
        )
        out.start()
        came = send(ev.at[:, pl.ds(0, 128)], r1.at[back], sem_1s.at[j], sem_1r.at[j], k, p * SIDE + back)
        first.append((out, came))
    own_first = pltpu.make_async_copy(ev.at[:, pl.ds(pl.multiple_of(q * 128, 128), 128)], r1.at[q], sem_1r.at[0])
    own_first.start()

    spread(2, gb)
    gsend = [
        send(gb, gx.at[pl.ds(HALO, LON)], sem_gs.at[0], sem_gr.at[0], before, t),
        send(gb.at[pl.ds(0, HALO)], gx.at[pl.ds(HALO + LON, HALO)], sem_gs.at[1], sem_gr.at[1], before, west),
        send(gb.at[pl.ds(LON - HALO, HALO)], gx.at[pl.ds(0, HALO)], sem_gs.at[2], sem_gr.at[2], before, east),
    ]
    for copy in gsend:
        copy.start()

    level_ids = lax.broadcasted_iota(jnp.int32, (LEV, LEV), 0)
    other_ids = lax.broadcasted_iota(jnp.int32, (LEV, LEV), 1)
    mixing = vmv[0] + jnp.where(level_ids == other_ids, 0.7, 0.0).astype(F32)
    for r in range(LEV):
        chosen = jnp.where(other_ids == (level_ids + r) % LEV, mixing, 0.0)
        mixf[r] = jnp.broadcast_to(jnp.sum(chosen, axis=1, keepdims=True), (LEV, LAT))
    mixb[0] = mixf[0]
    for r in range(1, LEV):
        mixb[r] = pltpu.roll(mixf[LEV - r], LEV - r, 0)
    lanes = lax.broadcasted_iota(jnp.int32, (LEV, LAT), 1)
    dn = jnp.where(lanes < LAT - 1, dfv[0], 0.0)
    dp = pltpu.roll(dn, 1, 1)
    latc[0] = dn
    latc[1] = dp
    latc[2] = 1.0 - dn - dp

    for copy in halo:
        copy.wait()

    def weigh(n, carry):
        cols = pl.ds(4 * n, 4)
        c = ac[1, cols]
        sq = c * c
        wts[0, cols] = (sq + c) * 0.5
        wts[1, cols] = 1.0 - sq
        wts[2, cols] = (sq - c) * 0.5
        return carry

    lax.fori_loop(0, 6, weigh, 0)

    def latitude(a):
        return latc[2] * a + latc[0] * pltpu.roll(a, LAT - 1, 2) + latc[1] * pltpu.roll(a, 1, 2)

    def couple(b, mix):
        total = mix[0] * b
        for r in range(1, LEV):
            total += mix[r] * pltpu.roll(b, LEV - r, 1)
        return total

    def forward(start, out):
        path = [(start, bufa, 0), (bufa, bufb, 0), (bufb, bufa, 0), (bufa, out, HALO)]
        for step, ((src, dst, off), blocks) in enumerate(zip(path, (6, 5, 5, 4))):

            def block(n, carry):
                i = step + 1 + 4 * n
                u = src[pl.ds(i - 1, 6)]
                a = wts[0, pl.ds(i, 4)] * u[0:4] + wts[1, pl.ds(i, 4)] * u[1:5] + wts[2, pl.ds(i, 4)] * u[2:6]
                dst[pl.ds(i - off, 4)] = couple(latitude(a), mixf)
                return carry

            lax.fori_loop(0, blocks, block, 0)

    def backward(start, out):
        path = [(start, bufa, 0), (bufa, bufb, 0), (bufb, bufa, 0), (bufa, out, HALO)]
        for step, ((src, dst, off), wide, narrow) in enumerate(zip(path, (6, 6, 5, 5), (6, 5, 5, 4))):

            def inner(n, carry):
                i = step + 4 * n
                bufg[pl.ds(i, 4)] = latitude(couple(src[pl.ds(i, 4)], mixb))
                return carry

            def outer(n, carry):
                i = step + 1 + 4 * n
                z = wts[1, pl.ds(i, 4)] * bufg[pl.ds(i, 4)]
                z += wts[0, pl.ds(i + 1, 4)] * bufg[pl.ds(i + 1, 4)]
                z += wts[2, pl.ds(i - 1, 4)] * bufg[pl.ds(i - 1, 4)]
                dst[pl.ds(i - off, 4)] = z
                return carry

            lax.fori_loop(0, wide, inner, 0)
            lax.fori_loop(0, narrow, outer, 0)

    forward(ac.at[0], mo.at[0])
    shift = [
        send(mo.at[0], ma, sem_ts.at[0], sem_tr.at[0], later, t),
        send(mo.at[1], mdd, sem_ts.at[1], sem_tr.at[1], later, t),
    ]
    shift[0].start()

    place = t % 4
    base = t - place
    for lt in range(LAT // 128):
        sl = pl.ds(lt * 128, 128)
        x = gb[:, :, sl]
        for n, off in ((8, 0), (4, 8), (2, 12), (1, 14)):
            pair = x.reshape(n, 2, LEV, 128)
            hb[pl.ds(off, n), :, sl] = pair[:, 0] - pair[:, 1]
            x = pair[:, 0] + pair[:, 1]
        cu[pl.ds(place, 1), :, sl] = x
    coarse = []
    for j in range(1, 4):
        peer, back = (place + j) % 4, (place + 4 - j) % 4
        out = send(cu.at[place], cu.at[place], sem_cs.at[j], sem_cr.at[j], k, base + peer)
        out.start()
        coarse.append((out, send(cu.at[place], cu.at[back], sem_cs.at[j], sem_cr.at[j], k, base + back)))

    own_first.wait()
    for out, came in first:
        out.wait_send()
        came.wait_recv()
    turned = jnp.transpose(r1[...].reshape(LAT, 128))
    s2[:, 0:LON, :] = turned.reshape(SIDE, LON, LAT)
    for g in range(2):
        rows = [s2[4 * g + j, 0:1, :] for j in range(4)]
        tops = jnp.concatenate(rows + [jnp.zeros((4, LAT), F32)], axis=0)
        for j in range(4):
            s2[4 * g + j, LON : LON + 8, :] = tops
    for s in range(SIDE):
        tile = q * SIDE + s
        out = send(s2.at[s], r2.at[p], sem_2s.at[s], sem_2r.at[p], k, tile)
        stay = pltpu.make_async_copy(s2.at[s], r2.at[p], sem_2r.at[p])

        @pl.when(tile != t)
        def _():
            out.start()

        @pl.when(tile == t)
        def _():
            stay.start()
            stay.wait()

    observe(ac[0, pl.ds(HALO, LON)], 3)
    q1 = obs[0] + obs[3]
    obs[3] = q1
    obs[4] = q1 / obs[1]
    spread(4, htq)

    for out, came in coarse:
        out.wait_send()
        came.wait_recv()
    for lev in range(LEV):
        came = send(s2.at[0], r2.at[lev], sem_2s.at[lev], sem_2r.at[lev], k, lev * SIDE + p)

        @pl.when(lev * SIDE + p != t)
        def _():
            came.wait_recv()

    vb[...] = jnp.swapaxes(r2[...], 0, 1)
    for lt in range(LAT // 128):
        sl = pl.ds(lt * 128, 128)
        u = [cu[j, :, sl] for j in range(4)]
        v = [vb[LON + j, :, sl] for j in range(4)]
        a0, d1, a2, d3 = u[0] + u[1], u[0] - u[1], u[2] + u[3], u[2] - u[3]
        top, bot = (a0 + a2) * v[0] * (1 / 64), (a0 - a2) * v[2] * (1 / 64)
        fine = jnp.where(place < 2, d1 * v[1], d3 * v[3]) * (1 / 32)
        x = jnp.where(place < 2, top + bot, top - bot) + jnp.where(place % 2 == 0, fine, -fine)
        x = x[None]
        for n, off, half in ((1, 14, 1 / 16), (2, 12, 1 / 8), (4, 8, 1 / 4), (8, 0, 1 / 2)):
            width = LON // n
            var = vb[pl.ds(0, LON), :, sl].reshape(n, width, LEV, 128)[:, width // 2]
            d = hb[pl.ds(off, n), :, sl] * var * half
            x = jnp.stack([x + d, x - d], axis=1).reshape(2 * n, LEV, 128)
        cb[:, :, sl] = x

    for copy in gsend:
        copy.wait()
    backward(gx, mtg)

    zero = jnp.zeros((LEV, LAT), F32)

    def fold(x):
        x = jnp.sum(x, axis=0, keepdims=True)
        return sum(x[:, n : n + 128] for n in range(0, x.shape[1], 128))

    def tile_of(num, den):
        row = lax.broadcasted_iota(jnp.int32, (8, 128), 0)
        return jnp.where(row == 0, num, jnp.where(row == 1, den, 0.0))

    def sum_start(which, stage, value):
        me = (q, p, k)[stage]
        arr[which, stage, me] = value
        pending = []
        for j in range(1, SIDE):
            peer, back = (me + j) % SIDE, (me + SIDE - j) % SIDE
            where = [(k, p * SIDE + peer), (k, peer * SIDE + q), (peer, t)][stage]
            whence = [(k, p * SIDE + back), (k, back * SIDE + q), (back, t)][stage]
            slot = arr.at[which, stage, me]
            sems = sem_as.at[which, stage, j], sem_ar.at[which, stage, j]
            out = send(slot, slot, *sems, *where)
            out.start()
            pending.append((out, send(slot, arr.at[which, stage, back], *sems, *whence)))
        return pending

    def sum_finish(which, stage, pending):
        for out, came in pending:
            out.wait_send()
            came.wait_recv()
        return jnp.sum(arr[which, stage], axis=0)

    def ratio(total):
        sums = jnp.sum(total, axis=1, keepdims=True)
        return sums[0:1] / (sums[1:2] + 1e-6)

    shift[0].wait()

    def differ(n, acc):
        cols = pl.ds(4 * n, 4)
        inside = pl.ds(4 * n + HALO, 4)
        a = ac[0, inside]
        b = a - jnp.where(k > 0, ma[cols], 0.0)
        bb[cols] = b
        dx[inside] = b - cb[cols]
        g = gb[cols]
        return acc[0] + jnp.sum(a * b, axis=0), acc[1] + jnp.sum(b * b + g * g, axis=0)

    num, den = lax.fori_loop(0, 4, differ, (zero, zero))
    edge = [
        send(dx.at[pl.ds(HALO, HALO)], dx.at[pl.ds(HALO + LON, HALO)], sem_hs.at[2], sem_hr.at[2], k, west),
        send(dx.at[pl.ds(LON, HALO)], dx.at[pl.ds(0, HALO)], sem_hs.at[3], sem_hr.at[3], k, east),
    ]
    for copy in edge:
        copy.start()
    q1 = obs[3]
    pending = sum_start(0, 0, tile_of(fold(num) + fold(obs[0] * q1), fold(den) + fold(q1 * q1)))

    observe(dx[pl.ds(HALO, LON)], 5)

    for copy in edge:
        copy.wait()
    forward(dx, mo.at[1])
    shift[1].start()

    total = sum_finish(0, 0, pending)
    pending = sum_start(0, 1, total)
    total = sum_finish(0, 1, pending)
    pending = sum_start(0, 2, total)
    total = sum_finish(0, 2, pending)
    al[0] = jnp.broadcast_to(ratio(total), (LEV, LAT))
    alpha = al[0]
    alpha1 = al[0, 0:1, 0:1]

    q1 = obs[3]
    q_obs = q1 - alpha1 * (q1 + obs[5])
    r_obs = obs[0] - alpha1 * q1

    def state_part(n, acc):
        cols = pl.ds(4 * n, 4)
        g = gb[cols]
        qs = g - alpha * (g - jnp.where(k < WINDOWS - 1, mtg[cols], 0.0) + htq[cols])
        return acc[0] - jnp.sum(alpha * g * qs, axis=0), acc[1] + jnp.sum(qs * qs, axis=0)

    acc = lax.fori_loop(0, 4, state_part, (zero, zero))
    shift[1].wait()

    def lam_part(n, acc):
        cols = pl.ds(4 * n, 4)
        inside = pl.ds(4 * n + HALO, 4)
        b = bb[cols]
        ql = b - alpha * (cb[cols] + dx[inside] - jnp.where(k > 0, mdd[cols], 0.0))
        rl = ac[0, inside] - alpha * b
        return acc[0] + jnp.sum(rl * ql, axis=0), acc[1] + jnp.sum(ql * ql, axis=0)

    num, den = lax.fori_loop(0, 4, lam_part, acc)
    total = tile_of(fold(num) + fold(r_obs * q_obs), fold(den) + fold(q_obs * q_obs))
    for stage in range(3):
        pending = sum_start(1, stage, total)
        total = sum_finish(1, stage, pending)
    beta = ratio(total)
    al[1] = jnp.broadcast_to(beta, (LEV, LAT))
    beta = al[1]

    def write(n, carry):
        cols = pl.ds(4 * n, 4)
        inside = pl.ds(4 * n + HALO, 4)
        a = ac[0, inside]
        mult[0, cols] = -(alpha * beta) * gb[cols]
        incr[0, cols] = alpha * a + beta * (a - alpha * dx[inside])
        return carry

    lax.fori_loop(0, 4, write, 0)
    beta1 = al[1, 0:1, 0:1]
    s1 = obs[2]
    omult[...] = alpha1 * s1 + beta1 * (s1 - alpha1 * obs[4])

    for s in range(SIDE):
        out = send(s2.at[s], r2.at[p], sem_2s.at[s], sem_2r.at[p], k, q * SIDE + s)

        @pl.when(q * SIDE + s != t)
        def _():
            out.wait_send()


def field(*lead):
    return pltpu.VMEM((*lead, LEV, LAT), F32)


SCRATCH = [
    field(2, WIDE),
    field(3, WIDE),
    pltpu.VMEM((LAT, SLOTS), BF16),
    pltpu.VMEM((LEV, SLOTS), jnp.int32),
    pltpu.VMEM((6, 1, SLOTS), F32),
    pltpu.VMEM((1, SLOTS), jnp.int32),
    pltpu.VMEM((LEV, SLOTS), F32),
    field(1),
    pltpu.VMEM((1, LEV, LEV), F32),
    field(3),
    field(LEV),
    field(LEV),
    field(LON),
    field(WIDE),
    field(WIDE),
    field(WIDE),
    field(WIDE),
    field(2, LON),
    field(LON),
    field(LON),
    field(LON),
    field(LON),
    field(LON),
    field(LON),
    field(WIDE),
    field(LON),
    field(4),
    pltpu.VMEM((SIDE, LAT // SIDE, 128), F32),
    pltpu.VMEM((SIDE, LON + 8, LAT), F32),
    pltpu.VMEM((LEV, LON + 8, LAT), F32),
    field(LON + 8),
    field(2),
    pltpu.VMEM((2, 3, SIDE, 8, 128), F32),
] + [
    pltpu.SemaphoreType.DMA(shape)
    for shape in (
        (8,), (4,), (4,), (8,), (8,), (8,), (8,), (4,), (4,), (3,), (3,), (2,), (2,), (2, 3, 8), (2, 3, 8),
    )
]


def body(md, od, ov, ow, oi, oc, cr, df, vm, ev):
    hbm = pl.BlockSpec(memory_space=pl.ANY)
    vmem = pl.BlockSpec(memory_space=pltpu.VMEM)
    return pl.pallas_call(
        kernel,
        out_shape=(
            jax.ShapeDtypeStruct((1, LON, LEV, LAT), F32),
            jax.ShapeDtypeStruct((1, SLOTS), F32),
            jax.ShapeDtypeStruct((1, LON, LEV, LAT), F32),
        ),
        in_specs=[hbm] * 5 + [pl.BlockSpec(memory_space=pltpu.SMEM)] + [hbm] * 4,
        out_specs=(vmem, vmem, vmem),
        scratch_shapes=SCRATCH,
        compiler_params=pltpu.CompilerParams(
            collective_id=0, has_side_effects=True, vmem_limit_bytes=48 * 1024 * 1024
        ),
        name="saddle",
    )(md[0], od, ov, ow[0], oi, oc, cr[0], df, vm, jnp.swapaxes(ev[0], 0, 1))


def solution(mesh):
    in_specs = (
        P("tm", "space", None, None),
        P("tm", "space"),
        P("tm", "space"),
        P("tm", None, "space"),
        P("tm", "space"),
        P("tm", "space"),
        P("tm", "space", None, None),
        P("tm", None, None),
        P("tm", None, None),
        P("tm", None, "space"),
    )
    out_specs = (P("tm", "space", None, None), P("tm", "space"), P("tm", "space", None, None))
    return jax.shard_map(body, mesh=mesh, in_specs=in_specs, out_specs=out_specs, check_vma=False)
```

time: 584 us -> 88 us (0.15)
  the two profiles are of different devices: /device:TPU:1 before, /device:TPU:8 now
where the time goes in v1:
time: 88 us; the launch traced here: 87.5 us
  Pallas kernels  77.8 us (88%)
  local copies, waits for them, and re-layouts  8.39 us (10%)
  between operations  1.32 us (2%)
    pallas_call x1, Pallas kernels, body(): pl.pallas_call(kernel, out_shape=(jax.ShapeDtypeStruct((1, LON, LEV, LAT)...  77.8 us
    unnamed x21, local copies, waits for them, and re-layouts  8.39 us

profile of v1, /device:TPU:8, one launch (start us, length us, event | category | flops | bytes accessed | tf_op | source)
XLA Modules:
  0.0 87.5 jit_solution(8182562065716294526)
XLA Ops:
  0.6 0.0 copy-start.5
  1.3 0.0 copy-done.5
  1.3 0.0 copy-start
  1.3 0.9 %copy-done = f32[1,16,8,384]{3,2,1,0:T(8,128)S(1)} copy-done((f32[1,16,8,384]{3,2,1,0:T(8,128)S(1)}, f32[1,16,8,384]{3,2,1,0:T(8,128)}, u32[]{:S(2)}) %copy-start) | copy-done | bytes 196632
  2.3 0.0 copy-start.1
  2.3 0.9 %copy-done.1 = f32[1,16,8,384]{3,2,1,0:T(8,128)S(1)} copy-done((f32[1,16,8,384]{3,2,1,0:T(8,128)S(1)}, f32[1,16,8,384]{3,2,1,0:T(8,128)}, u32[]{:S(2)}) %copy-start.1) | copy-done | bytes 196632
  3.2 0.0 copy-start.2
  3.2 0.9 %copy-done.2 = f32[1,1024,48]{1,2,0:T(8,128)S(1)} copy-done((f32[1,1024,48]{1,2,0:T(8,128)S(1)}, f32[1,1024,48]{1,2,0:T(8,128)}, u32[]{:S(2)}) %copy-start.2) | copy-done | bytes 196632
  4.1 0.0 copy-start.3
  4.1 0.8 copy-done.3
  5.0 0.0 copy-start.4
  5.0 0.7 copy-done.4
  5.7 0.0 copy-start.6
  5.7 0.7 copy-done.6
  6.4 0.0 copy-start.7
  6.4 0.7 copy-done.7
  7.1 0.0 copy-start.8
  7.1 0.7 copy-done.8
  7.7 77.8 %saddle.1 = (f32[1,16,8,384]{3,2,1,0:T(8,128)S(1)}, f32[1,2048]{1,0:T(1,128)S(1)}, f32[1,16,8,384]{3,2,1,0:T(8,128)S(1)}) custom-call(f32[16,8,384]{2,1,0:T(8,128)S(1)} %bitcast.6, f32[1,2048]{1,0:T(1,128)S(1)} %copy-done.5, f32[1,2048]{1,0:T(1,128)S(1)} %copy-done.6, f32[8,2048]{1,0:T(8,128)S(1)} %bitcast.9, s32[1,2048]{1,0:T(1,128)S(1)} %copy-done.7, ...), custom_call_target="tpu_custom_call" | custom-call | tf_op jit(solution)/shard_map/saddle/pallas_call | solution.py:484
  85.6 0.7 copy.17
  86.3 0.6 copy.18
  86.9 0.7 copy.19
Async XLA Ops:
  0.6 0.7 copy-start.5
  1.3 0.9 %copy-start = (f32[1,16,8,384]{3,2,1,0:T(8,128)S(1)}, f32[1,16,8,384]{3,2,1,0:T(8,128)}, u32[]{:S(2)}) copy-start(f32[1,16,8,384]{3,2,1,0:T(8,128)} %param.10) | copy-start | bytes 589828
  2.3 0.9 %copy-start.1 = (f32[1,16,8,384]{3,2,1,0:T(8,128)S(1)}, f32[1,16,8,384]{3,2,1,0:T(8,128)}, u32[]{:S(2)}) copy-start(f32[1,16,8,384]{3,2,1,0:T(8,128)} %param.16) | copy-start | bytes 589828
  3.2 0.9 %copy-start.2 = (f32[1,1024,48]{1,2,0:T(8,128)S(1)}, f32[1,1024,48]{1,2,0:T(8,128)}, u32[]{:S(2)}) copy-start(f32[1,1024,48]{1,2,0:T(8,128)} %param.19) | copy-start | bytes 589828
  4.1 0.8 copy-start.3
  5.0 0.7 copy-start.4
  5.7 0.7 copy-start.6
  6.4 0.7 copy-start.7
  7.1 0.7 copy-start.8

commit v2 on v1

v2 whole, which is shorter than its diff:
```python
import jax
import jax.numpy as jnp
from jax import lax
from jax.experimental import pallas as pl
from jax.experimental.pallas import tpu as pltpu
from jax.sharding import PartitionSpec as P

MESH = pl.DeviceIdType.MESH
F32 = jnp.float32
BF16 = jnp.bfloat16
LON, LEV, LAT, SLOTS = 16, 8, 384, 2048
WINDOWS, TILES, SIDE = 8, 64, 8
HALO = 4
WIDE = LON + 2 * HALO + 2
CHUNK = 512
FAR_FIRST = (4, 3, 5, 2, 6, 1, 7)


def kernel(
    md, od, ov, ow, oi, oc, cr, df, vm, ev,
    mult, omult, incr,
    ac, wts, onehot, lonb, obs, oiv, ocv, wv, dfv, vmv, latc, mixf, mixb,
    gb, gx, bufa, bufb, bufg, mo, ma, an, mtg, htq, bb, cb, dx,
    hb, cu, evv, evp, r1, tops, s2, r2, vt, vb, al, arr,
    sem_load, sem_hs, sem_hr, sem_1s, sem_1r, sem_2s, sem_2r, sem_cs, sem_cr, sem_gs, sem_gr, sem_ts, sem_tr, sem_as, sem_ar,
):
    k = lax.axis_index("tm")
    t = lax.axis_index("space")
    x, zl = k // 2, k % 2
    zh, y, c = t // 16, t // 2 % 8, t % 2
    east, west = (t + 1) % TILES, (t + TILES - 1) % TILES
    later, before = (k + 1) % WINDOWS, (k + WINDOWS - 1) % WINDOWS
    place = t % 4
    base = t - place

    def send(src, dst, ssem, rsem, kk, tt):
        return pltpu.make_async_remote_copy(
            src_ref=src, dst_ref=dst, send_sem=ssem, recv_sem=rsem, device_id=(kk, tt), device_id_type=MESH
        )

    def tile_at(zz, yy, cc):
        return zz * 16 + yy * 2 + cc

    def on_y(place):
        return k, tile_at(zh, place, c)

    def on_z(place):
        return x * 2 + place % 2, tile_at(place // 2, y, c)

    def on_xc(place):
        return place // 2 * 2 + zl, tile_at(zh, y, place % 2)

    def on_zc(place):
        return k, tile_at(place // 2, y, place % 2)

    loads = [
        pltpu.make_async_copy(src, dst, sem_load.at[n])
        for n, (src, dst) in enumerate(
            [
                (ev, evv),
                (oi, oiv),
                (od, obs.at[0]),
                (ov, obs.at[1]),
                (oc, ocv),
                (ow, wv),
                (md, ac.at[0, pl.ds(HALO, LON)]),
                (cr, ac.at[1, pl.ds(HALO, LON)]),
                (df, dfv),
                (vm, vmv),
            ]
        )
    ]
    for load in loads:
        load.start()

    barrier = pltpu.get_barrier_semaphore()

    def greet(kk, tt):
        pl.semaphore_signal(barrier, inc=1, device_id=(kk, tt), device_id_type=MESH)

    for j in FAR_FIRST:
        greet(*on_y((y + j) % SIDE))
        greet(*on_zc((zh * 2 + c + j) % SIDE))
    for j in range(4):
        greet(x * 2 + 1 - zl, tile_at((zh + j) % 4, y, c))
    for j in range(1, 4):
        greet((x + j) % 4 * 2 + zl, t)
        greet((x + j) % 4 * 2 + zl, t + 1 - 2 * c)
    greet(later, east)
    greet(later, west)
    greet(later, t)
    greet(before, t)
    greet(k, base + 3 - place)
    greet(k, east)
    greet(k, west)

    lane = lax.broadcasted_iota(jnp.int32, (LAT // SIDE, 128), 1)
    loads[0].wait()
    for zz in range(4):
        for cc in range(2):
            block = None
            for yy in range(SIDE):
                source = evv[:, pl.ds((zz * 2 + yy // 4) * 128, 128)]
                offset = (yy * 16 - (yy % 4 * 32 + cc * 16)) % 128
                moved = pltpu.roll(source, offset, 1) if offset else source
                block = moved if block is None else jnp.where(lane >= yy * 16, moved, block)
            evp[zz * 2 + cc] = block
    for load in loads[1:]:
        load.wait()

    index = oiv[...]
    lon = (index * 10923) >> 22
    lat = index - lon * LAT
    lonb[...] = jnp.broadcast_to(lon, (LEV, SLOTS))
    for n in range(SLOTS // CHUNK):
        cols = pl.ds(n * CHUNK, CHUNK)
        rows = lax.broadcasted_iota(jnp.int32, (LAT, CHUNK), 0)
        onehot[:, cols] = jnp.where(rows == lat[:, n * CHUNK : (n + 1) * CHUNK], 1.0, 0.0).astype(BF16)
    live = lax.broadcasted_iota(jnp.int32, (1, SLOTS), 1) < ocv[...]
    o0 = jnp.where(live, obs[0], 0.0)
    s1 = o0 / obs[1]
    obs[0] = o0
    obs[2] = s1

    def pieces(x):
        high = x.astype(BF16)
        return high, (x - high.astype(F32)).astype(BF16)

    def spread(row, out):
        total = jnp.zeros((LON * LEV, LAT), F32)
        for n in range(SLOTS // CHUNK):
            cols = pl.ds(n * CHUNK, CHUNK)
            terms = wv[:, cols] * obs[row, :, cols]
            ids = lax.broadcasted_iota(jnp.int32, (LON, LEV, CHUNK), 0)
            placed = jnp.where(ids == lonb[:, cols][None], terms[None], 0.0).reshape(LON * LEV, CHUNK)
            for piece in pieces(placed):
                total += lax.dot_general(piece, onehot[:, cols], (((1,), (1,)), ((), ())), preferred_element_type=F32)
        out[...] = total.reshape(LON, LEV, LAT)

    def observe(field, row):
        high, low = pieces(field.reshape(LON * LEV, LAT))
        for n in range(SLOTS // CHUNK):
            cols = pl.ds(n * CHUNK, CHUNK)
            picked = jnp.dot(high, onehot[:, cols], preferred_element_type=F32)
            picked += jnp.dot(low, onehot[:, cols], preferred_element_type=F32)
            picked = picked.reshape(LON, LEV, CHUNK)
            here = lonb[:, cols]
            column = jnp.zeros((LEV, CHUNK), F32)
            for i in range(LON):
                column = jnp.where(here == i, picked[i], column)
            total = jnp.sum(column * wv[:, cols], axis=0, keepdims=True)
            slot = lax.broadcasted_iota(jnp.int32, (1, CHUNK), 1) + n * CHUNK
            obs[row, :, cols] = jnp.where(slot < ocv[...], total, 0.0)

    spread(2, gb)
    for lt in range(LAT // 128):
        sl = pl.ds(lt * 128, 128)
        u = gb[:, :, sl]
        for n, off in ((8, 0), (4, 8), (2, 12), (1, 14)):
            pair = u.reshape(n, 2, LEV, 128)
            hb[pl.ds(off, n), :, sl] = pair[:, 0] - pair[:, 1]
            u = pair[:, 0] + pair[:, 1]
        cu[pl.ds(place, 1), :, sl] = u

    level_ids = lax.broadcasted_iota(jnp.int32, (LEV, LEV), 0)
    other_ids = lax.broadcasted_iota(jnp.int32, (LEV, LEV), 1)
    mixing = vmv[0] + jnp.where(level_ids == other_ids, 0.7, 0.0).astype(F32)
    for r in range(LEV):
        chosen = jnp.where(other_ids == (level_ids + r) % LEV, mixing, 0.0)
        mixf[r] = jnp.broadcast_to(jnp.sum(chosen, axis=1, keepdims=True), (LEV, LAT))
    mixb[0] = mixf[0]
    for r in range(1, LEV):
        mixb[r] = pltpu.roll(mixf[LEV - r], LEV - r, 0)
    lanes = lax.broadcasted_iota(jnp.int32, (LEV, LAT), 1)
    dn = jnp.where(lanes < LAT - 1, dfv[0], 0.0)
    dp = pltpu.roll(dn, 1, 1)
    latc[0] = dn
    latc[1] = dp
    latc[2] = 1.0 - dn - dp

    def weigh(start, count):
        cols = pl.ds(start, count)
        c = ac[1, cols]
        sq = c * c
        wts[0, cols] = (sq + c) * 0.5
        wts[1, cols] = 1.0 - sq
        wts[2, cols] = (sq - c) * 0.5

    for n in range(4):
        weigh(HALO + 4 * n, 4)

    pl.semaphore_wait(barrier, 31)

    halo = [
        send(ac.at[:, pl.ds(HALO, HALO)], ac.at[:, pl.ds(HALO + LON, HALO)], sem_hs.at[0], sem_hr.at[0], k, west),
        send(ac.at[:, pl.ds(LON, HALO)], ac.at[:, pl.ds(0, HALO)], sem_hs.at[1], sem_hr.at[1], k, east),
    ]
    for copy in halo:
        copy.start()

    me = zh * 2 + c
    first = []
    for j in FAR_FIRST:
        peer, back = (me + j) % SIDE, (me + SIDE - j) % SIDE
        out = send(evp.at[peer], r1.at[me], sem_1s.at[j], sem_1r.at[j], *on_zc(peer))
        out.start()
        first.append((out, send(evp.at[peer], r1.at[back], sem_1s.at[j], sem_1r.at[j], *on_zc(back))))
    r1[pl.ds(me, 1)] = evp[pl.ds(me, 1)]

    coarse = []
    for j in range(1, 4):
        peer, back = (place + j) % 4, (place + 4 - j) % 4
        out = send(cu.at[place], cu.at[place], sem_cs.at[j], sem_cr.at[j], k, base + peer)
        out.start()
        coarse.append((out, send(cu.at[place], cu.at[back], sem_cs.at[j], sem_cr.at[j], k, base + back)))
    gsend = [
        send(gb, gx.at[pl.ds(HALO, LON)], sem_gs.at[0], sem_gr.at[0], before, t),
        send(gb.at[pl.ds(0, HALO)], gx.at[pl.ds(HALO + LON, HALO)], sem_gs.at[1], sem_gr.at[1], before, west),
        send(gb.at[pl.ds(LON - HALO, HALO)], gx.at[pl.ds(0, HALO)], sem_gs.at[2], sem_gr.at[2], before, east),
    ]
    asend = send(ac.at[0, pl.ds(HALO, LON)], an, sem_ts.at[1], sem_tr.at[1], before, t)
    for copy in gsend:
        copy.start()

    observe(ac[0, pl.ds(HALO, LON)], 3)
    q1 = obs[0] + obs[3]
    obs[3] = q1
    obs[4] = q1 / obs[1]

    def latitude(a):
        return latc[2] * a + latc[0] * pltpu.roll(a, LAT - 1, 2) + latc[1] * pltpu.roll(a, 1, 2)

    def couple(b, mix):
        total = mix[0] * b
        for r in range(1, LEV):
            total += mix[r] * pltpu.roll(b, LEV - r, 1)
        return total

    def forward(start, out):
        path = [(start, bufa, 0), (bufa, bufb, 0), (bufb, bufa, 0), (bufa, out, HALO)]
        for step, ((src, dst, off), blocks) in enumerate(zip(path, (6, 5, 5, 4))):

            def block(n, carry):
                i = step + 1 + 4 * n
                u = src[pl.ds(i - 1, 6)]
                a = wts[0, pl.ds(i, 4)] * u[0:4] + wts[1, pl.ds(i, 4)] * u[1:5] + wts[2, pl.ds(i, 4)] * u[2:6]
                dst[pl.ds(i - off, 4)] = couple(latitude(a), mixf)
                return carry

            lax.fori_loop(0, blocks, block, 0, unroll=True)

    def backward(start, out):
        path = [(start, bufa, 0), (bufa, bufb, 0), (bufb, bufa, 0), (bufa, out, HALO)]
        for step, ((src, dst, off), wide, narrow) in enumerate(zip(path, (6, 6, 5, 5), (6, 5, 5, 4))):

            def inner(n, carry):
                i = step + 4 * n
                bufg[pl.ds(i, 4)] = latitude(couple(src[pl.ds(i, 4)], mixb))
                return carry

            def outer(n, carry):
                i = step + 1 + 4 * n
                z = wts[1, pl.ds(i, 4)] * bufg[pl.ds(i, 4)]
                z += wts[0, pl.ds(i + 1, 4)] * bufg[pl.ds(i + 1, 4)]
                z += wts[2, pl.ds(i - 1, 4)] * bufg[pl.ds(i - 1, 4)]
                dst[pl.ds(i - off, 4)] = z
                return carry

            lax.fori_loop(0, wide, inner, 0, unroll=True)
            lax.fori_loop(0, narrow, outer, 0, unroll=True)

    for copy in halo:
        copy.wait()
    weigh(0, HALO)
    weigh(HALO + LON, HALO)
    forward(ac.at[0], mo.at[0])
    shift = send(mo.at[0], ma, sem_ts.at[0], sem_tr.at[0], later, t)
    shift.start()
    asend.start()

    for out, came in first:
        came.wait_recv()
    turned = jnp.transpose(r1[...].reshape(LAT, 128))
    s2[:, 0:LON, :] = turned.reshape(SIDE, LON, LAT)
    tops[0] = jnp.concatenate([turned[n * LON : n * LON + 1] for n in range(SIDE)], axis=0)
    swap = send(tops.at[0], tops.at[1], sem_cs.at[0], sem_cr.at[0], k, t + 1 - 2 * c)
    swap.start()
    swap.wait()
    even = jnp.where(c == 0, tops[0], tops[1])
    odd = jnp.where(c == 0, tops[1], tops[0])
    for n in range(0, SIDE, 2):
        rows = [even[n : n + 1], odd[n : n + 1], even[n + 1 : n + 2], odd[n + 1 : n + 2], jnp.zeros((4, LAT), F32)]
        rows = jnp.concatenate(rows, axis=0)
        s2[n, LON : LON + 8, :] = rows
        s2[n + 1, LON : LON + 8, :] = rows
    second = []
    for j in FAR_FIRST:
        peer, back = (y + j) % SIDE, (y + SIDE - j) % SIDE
        out = send(s2.at[peer], r2.at[y], sem_2s.at[j], sem_2r.at[j], *on_y(peer))
        out.start()
        second.append((out, send(s2.at[peer], r2.at[back], sem_2s.at[j], sem_2r.at[j], *on_y(back))))
    r2[pl.ds(y, 1)] = s2[pl.ds(y, 1)]

    spread(4, htq)
    for copy in gsend:
        copy.wait()
    backward(gx, mtg)

    for out, came in coarse:
        came.wait_recv()
    for out, came in second:
        came.wait_recv()
    lane = lax.broadcasted_iota(jnp.int32, (LON + 8, LAT), 1)
    for zz in range(4):
        for half in range(2):
            level = None
            for m in range(4):
                offset = (96 * (m - zz)) % LAT
                source = r2[half * 4 + m]
                moved = pltpu.roll(source, offset, 1) if offset else source
                level = moved if level is None else jnp.where(lane >= 96 * m, moved, level)
            vt[zz * 2 + half] = level
    vb[...] = jnp.swapaxes(vt[...], 0, 1)
    for lt in range(LAT // 128):
        sl = pl.ds(lt * 128, 128)
        u = [cu[j, :, sl] for j in range(4)]
        v = [vb[LON + j, :, sl] for j in range(4)]
        a0, d1, a2, d3 = u[0] + u[1], u[0] - u[1], u[2] + u[3], u[2] - u[3]
        top, bot = (a0 + a2) * v[0] * (1 / 64), (a0 - a2) * v[2] * (1 / 64)
        fine = jnp.where(place < 2, d1 * v[1], d3 * v[3]) * (1 / 32)
        u = jnp.where(place < 2, top + bot, top - bot) + jnp.where(place % 2 == 0, fine, -fine)
        u = u[None]
        for n, off, half in ((1, 14, 1 / 16), (2, 12, 1 / 8), (4, 8, 1 / 4), (8, 0, 1 / 2)):
            width = LON // n
            var = vb[pl.ds(0, LON), :, sl].reshape(n, width, LEV, 128)[:, width // 2]
            d = hb[pl.ds(off, n), :, sl] * var * half
            u = jnp.stack([u + d, u - d], axis=1).reshape(2 * n, LEV, 128)
        cb[:, :, sl] = u

    shift.wait()

    def differ(n, carry):
        cols = pl.ds(4 * n, 4)
        inside = pl.ds(4 * n + HALO, 4)
        dx[inside] = ac[0, inside] - jnp.where(k > 0, ma[cols], 0.0) - cb[cols]
        return carry

    lax.fori_loop(0, 4, differ, 0, unroll=True)
    edge = [
        send(dx.at[pl.ds(HALO, HALO)], dx.at[pl.ds(HALO + LON, HALO)], sem_hs.at[2], sem_hr.at[2], k, west),
        send(dx.at[pl.ds(LON, HALO)], dx.at[pl.ds(0, HALO)], sem_hs.at[3], sem_hr.at[3], k, east),
    ]
    for copy in edge:
        copy.start()
    observe(dx[pl.ds(HALO, LON)], 5)

    def fold(x):
        x = jnp.sum(x, axis=0, keepdims=True)
        return sum(x[:, n : n + 128] for n in range(0, x.shape[1], 128))

    zero = jnp.zeros((LEV, LAT), F32)

    def state_part(n, acc):
        cols = pl.ds(4 * n, 4)
        g = gb[cols]
        f = g - jnp.where(k < WINDOWS - 1, mtg[cols], 0.0) + htq[cols]
        return acc[0] + jnp.sum(g * g, axis=0), acc[1] + jnp.sum(g * f, axis=0), acc[2] + jnp.sum(f * f, axis=0)

    gg, gf, ff = lax.fori_loop(0, 4, state_part, (zero, zero, zero), unroll=True)
    o0, q1 = obs[0], obs[3]
    h = q1 + obs[5]
    sums = [fold(o0 * q1), fold(gg) + fold(q1 * q1), fold(o0 * h), fold(gf) + fold(q1 * h), fold(ff) + fold(h * h)]
    asend.wait()

    for copy in edge:
        copy.wait()
    forward(dx, mo.at[1])

    def lam_part(n, acc):
        cols = pl.ds(4 * n, 4)
        a = an[cols]
        b = a - jnp.where(k < WINDOWS - 1, mo[0, cols], 0.0)
        e = b - jnp.where(k < WINDOWS - 1, mo[1, cols], 0.0)
        products = (a * b, b * b, a * e, b * e, e * e)
        return tuple(total + jnp.sum(product, axis=0) for total, product in zip(acc, products))

    acc = lax.fori_loop(0, 4, lam_part, (zero,) * 5, unroll=True)
    row = lax.broadcasted_iota(jnp.int32, (8, 128), 0)
    total = jnp.zeros((8, 128), F32)
    for n in range(5):
        total = jnp.where(row == n, sums[n] + fold(acc[n]), total)

    sent = []
    for stage, (me, ring) in enumerate(((y, on_y), (zh * 2 + zl, on_z), (x * 2 + c, on_xc))):
        arr[stage, me] = total
        pending = []
        for j in FAR_FIRST:
            peer, back = (me + j) % SIDE, (me + SIDE - j) % SIDE
            slot = arr.at[stage, me]
            sems = sem_as.at[stage, j], sem_ar.at[stage, j]
            out = send(slot, slot, *sems, *ring(peer))
            out.start()
            sent.append(out)
            pending.append(send(slot, arr.at[stage, back], *sems, *ring(back)))
        for came in pending:
            came.wait_recv()
        total = jnp.sum(arr[stage], axis=0)
    total = jnp.sum(total, axis=1, keepdims=True)
    rq, qq, re, qe, ee = (total[n : n + 1] for n in range(5))
    alpha = rq / (qq + 1e-6)
    beta = alpha * (1e-6 - re + alpha * qe) / (qq - 2.0 * alpha * qe + alpha * alpha * ee + 1e-6)
    al[0] = jnp.broadcast_to(alpha, (LEV, LAT))
    al[1] = jnp.broadcast_to(beta, (LEV, LAT))
    alpha, beta = al[0], al[1]

    def write(n, carry):
        cols = pl.ds(4 * n, 4)
        inside = pl.ds(4 * n + HALO, 4)
        a = ac[0, inside]
        mult[0, cols] = -(alpha * beta) * gb[cols]
        incr[0, cols] = alpha * a + beta * (a - alpha * dx[inside])
        return carry

    lax.fori_loop(0, 4, write, 0, unroll=True)
    alpha, beta = al[0, 0:1, 0:1], al[1, 0:1, 0:1]
    s1 = obs[2]
    omult[...] = alpha * s1 + beta * (s1 - alpha * obs[4])

    for out, came in first + second + coarse:
        out.wait_send()
    for out in sent:
        out.wait_send()


def field(*lead):
    return pltpu.VMEM((*lead, LEV, LAT), F32)


SCRATCH = [
    field(2, WIDE),
    field(3, WIDE),
    pltpu.VMEM((LAT, SLOTS), BF16),
    pltpu.VMEM((LEV, SLOTS), jnp.int32),
    pltpu.VMEM((6, 1, SLOTS), F32),
    pltpu.VMEM((1, SLOTS), jnp.int32),
    pltpu.VMEM((1, 1), jnp.int32),
    pltpu.VMEM((LEV, SLOTS), F32),
    field(1),
    pltpu.VMEM((1, LEV, LEV), F32),
    field(3),
    field(LEV),
    field(LEV),
    field(LON),
    field(WIDE),
    field(WIDE),
    field(WIDE),
    field(WIDE),
    field(2, LON),
    field(LON),
    field(LON),
    field(LON),
    field(LON),
    field(LON),
    field(LON),
    field(WIDE),
    field(LON),
    field(4),
    pltpu.VMEM((LAT // SIDE, TILES * LON), F32),
    pltpu.VMEM((SIDE, LAT // SIDE, 128), F32),
    pltpu.VMEM((SIDE, LAT // SIDE, 128), F32),
    field(2),
    pltpu.VMEM((SIDE, LON + 8, LAT), F32),
    pltpu.VMEM((SIDE, LON + 8, LAT), F32),
    pltpu.VMEM((LEV, LON + 8, LAT), F32),
    field(LON + 8),
    field(2),
    pltpu.VMEM((3, SIDE, 8, 128), F32),
] + [
    pltpu.SemaphoreType.DMA(shape)
    for shape in (
        (10,), (4,), (4,), (8,), (8,), (8,), (8,), (4,), (4,), (3,), (3,), (2,), (2,), (3, 8), (3, 8),
    )
]


def body(md, od, ov, ow, oi, oc, cr, df, vm, ev):
    hbm = pl.BlockSpec(memory_space=pltpu.HBM)
    vmem = pl.BlockSpec(memory_space=pltpu.VMEM)
    return pl.pallas_call(
        kernel,
        out_shape=(
            jax.ShapeDtypeStruct((1, LON, LEV, LAT), F32),
            jax.ShapeDtypeStruct((1, SLOTS), F32),
            jax.ShapeDtypeStruct((1, LON, LEV, LAT), F32),
        ),
        in_specs=[hbm] * 10,
        out_specs=(vmem, vmem, vmem),
        scratch_shapes=SCRATCH,
        compiler_params=pltpu.CompilerParams(
            collective_id=0, has_side_effects=True, vmem_limit_bytes=60 * 1024 * 1024
        ),
        name="saddle",
    )(md[0], od, ov, ow[0], oi, oc, cr[0], df, vm, jnp.swapaxes(ev[0], 0, 1))


def solution(mesh):
    in_specs = (
        P("tm", "space", None, None),
        P("tm", "space"),
        P("tm", "space"),
        P("tm", None, "space"),
        P("tm", "space"),
        P("tm", "space"),
        P("tm", "space", None, None),
        P("tm", None, None),
        P("tm", None, None),
        P("tm", None, "space"),
    )
    out_specs = (P("tm", "space", None, None), P("tm", "space"), P("tm", "space", None, None))
    return jax.shard_map(body, mesh=mesh, in_specs=in_specs, out_specs=out_specs, check_vma=False)
```

time: 88 us -> 58 us (0.66)
  the two profiles are of different devices: /device:TPU:8 before, /device:TPU:1 now
where the time goes in v2:
time: 58 us; the launch traced here: 57.8 us
  Pallas kernels  53.6 us (92%)
  local copies, waits for them, and re-layouts  2.94 us (5%)
  between operations  1.3 us (2%)
    pallas_call x1, Pallas kernels, body(): pl.pallas_call(kernel, out_shape=(jax.ShapeDtypeStruct((1, LON, LEV, LAT)...  53.6 us
    unnamed x7, local copies, waits for them, and re-layouts  2.94 us

profile of v2, /device:TPU:1, one launch (start us, length us, event | category | flops | bytes accessed | tf_op | source)
XLA Modules:
  0.0 57.8 jit_solution(11257472929054106559)
XLA Ops:
  1.3 53.6 %saddle.1 = (f32[1,16,8,384]{3,2,1,0:T(8,128)}, f32[1,2048]{1,0:T(1,128)}, f32[1,16,8,384]{3,2,1,0:T(8,128)}) custom-call(f32[16,8,384]{2,1,0:T(8,128)} %bitcast.6, f32[1,2048]{1,0:T(1,128)} %od.1, f32[1,2048]{1,0:T(1,128)} %ov.1, f32[8,2048]{1,0:T(8,128)} %bitcast.9, s32[1,2048]{1,0:T(1,128)} %oi.1, s32[1,1]{1,0:T(1,128)S(6)} %copy.16.oc, ...), custom_call_target="tpu_custom_call" | custom-call | tf_op jit(solution)/shard_map/saddle/pallas_call | solution.py:489
  54.9 0.0 copy-start.1
  54.9 0.0 copy-start
  54.9 1.7 %copy.17 = f32[1,16,8,384]{3,2,1,0:T(8,128)} copy(f32[1,16,8,384]{3,2,1,0:T(8,128)} %get-tuple-element.6) | data formatting | bytes 393216
  56.6 0.0 copy-done.1
  56.6 0.6 %copy.18 = f32[1,2048]{1,0:T(1,128)} copy(f32[1,2048]{1,0:T(1,128)S(1)} %copy-done.1) | data formatting | bytes 16384
  57.2 0.0 copy-done
  57.2 0.7 %copy.19 = f32[1,16,8,384]{3,2,1,0:T(8,128)} copy(f32[1,16,8,384]{3,2,1,0:T(8,128)S(1)} %copy-done) | data formatting | bytes 393216
Async XLA Ops:
  54.9 1.7 %copy-start.1 = (f32[1,2048]{1,0:T(1,128)S(1)}, f32[1,2048]{1,0:T(1,128)}, u32[]{:S(2)}) copy-start(f32[1,2048]{1,0:T(1,128)} %get-tuple-element.7) | copy-start | bytes 24580
  54.9 2.3 %copy-start = (f32[1,16,8,384]{3,2,1,0:T(8,128)S(1)}, f32[1,16,8,384]{3,2,1,0:T(8,128)}, u32[]{:S(2)}) copy-start(f32[1,16,8,384]{3,2,1,0:T(8,128)} %get-tuple-element.8) | copy-start | bytes 589828

commit v3 on v2

v3 whole, which is shorter than its diff:
```python
import jax
import jax.numpy as jnp
from jax import lax
from jax.experimental import pallas as pl
from jax.experimental.pallas import tpu as pltpu
from jax.sharding import PartitionSpec as P

MESH = pl.DeviceIdType.MESH
F32 = jnp.float32
BF16 = jnp.bfloat16
LON, LEV, LAT, SLOTS = 16, 8, 384, 2048
WINDOWS, TILES, SIDE = 8, 64, 8
HALO = 4
WIDE = LON + 2 * HALO + 2
CHUNK = 512
FAR_FIRST = (4, 3, 5, 2, 6, 1, 7)
FAR_YC = (8, 7, 9, 6, 10, 5, 11, 4, 12, 3, 13, 2, 14, 1, 15)
FAR_ZX = tuple(sorted(range(1, 32), key=lambda j: (-min(j // 4, 8 - j // 4), j)))


def kernel(
    md, od, ov, ow, oi, oc, cr, df, vm, ev,
    gb, dd, ao, so, al,
    ac, wts, onehot, onehot_n, lonb, lonb_n, obs, oiv, oiv_n, wv, terms, terms_n, dfv, vmv, latc, mixf, mixb,
    gx, bufa, bufb, bufg, mo, ma, an, mtg, htq, dx,
    hb, cu, evv, evp, r1, s2, r2, vt, vb, wq, wn, up, arr1, arr2,
    sem_load, sem_hs, sem_hr, sem_1s, sem_1r, sem_2s, sem_2r, sem_ws, sem_wr, sem_cs, sem_cr, sem_gs, sem_gr, sem_ts, sem_tr, sem_a,
):
    k = lax.axis_index("tm")
    t = lax.axis_index("space")
    x, zl = k // 2, k % 2
    zh, y, c = t // 16, t // 2 % 8, t % 2
    east, west = (t + 1) % TILES, (t + TILES - 1) % TILES
    later, before = (k + 1) % WINDOWS, (k + WINDOWS - 1) % WINDOWS
    place = t % 4
    base = t - place

    def send(src, dst, ssem, rsem, kk, tt):
        return pltpu.make_async_remote_copy(
            src_ref=src, dst_ref=dst, send_sem=ssem, recv_sem=rsem, device_id=(kk, tt), device_id_type=MESH
        )

    def tile_at(zz, yy, cc):
        return zz * 16 + yy * 2 + cc

    def on_y(place):
        return k, tile_at(zh, place, c)

    def on_zc(place):
        return k, tile_at(place // 2, y, place % 2)

    def on_yc(place):
        return k, tile_at(zh, place // 2, place % 2)

    def on_zx(place):
        return place % 4 * 2 + place // 4 % 2, tile_at(place // 8, y, c)

    loads = [
        pltpu.make_async_copy(src, dst, sem_load.at[n])
        for n, (src, dst) in enumerate(
            [
                (ev, evv),
                (md, ac.at[0, pl.ds(HALO, LON)]),
                (cr, ac.at[1, pl.ds(HALO, LON)]),
                (oi, oiv),
                (od, obs.at[0]),
                (ov, obs.at[1]),
                (ow, wv),
                (df, dfv),
                (vm, vmv),
            ]
        )
    ]
    for load in loads:
        load.start()

    barrier = pltpu.get_barrier_semaphore()

    def greet(kk, tt):
        pl.semaphore_signal(barrier, inc=1, device_id=(kk, tt), device_id_type=MESH)

    me_yc, me_zx = y * 2 + c, (zh * 2 + zl) * 4 + x
    for j in FAR_ZX:
        greet(*on_zx((me_zx + j) % 32))
    for j in FAR_YC:
        greet(*on_yc((me_yc + j) % 16))
    for j in range(1, 4):
        greet(k, tile_at((zh + j) % 4, y, 1 - c))
    greet(k, east)
    greet(k, west)
    beside = jnp.where(place == 0, base + TILES - 4, base + 4) % TILES

    @pl.when((place == 0) | (place == 3))
    def _():
        for j in range(4):
            greet(k, beside + j)


    lane_v = lax.broadcasted_iota(jnp.int32, (LAT // SIDE, 128), 1)
    loads[0].wait()
    for zz in range(4):
        for cc in range(2):
            block = None
            for yy in range(SIDE):
                source = evv[:, pl.ds((zz * 2 + yy // 4) * 128, 128)]
                offset = (yy * 16 - (yy % 4 * 32 + cc * 16)) % 128
                moved = pltpu.roll(source, offset, 1) if offset else source
                block = moved if block is None else jnp.where(lane_v >= yy * 16, moved, block)
            evp[zz * 2 + cc] = block
    halo = [
        send(ac.at[:, pl.ds(HALO, HALO)], ac.at[:, pl.ds(HALO + LON, HALO)], sem_hs.at[0], sem_hr.at[0], k, west),
        send(ac.at[:, pl.ds(LON, HALO)], ac.at[:, pl.ds(0, HALO)], sem_hs.at[1], sem_hr.at[1], k, east),
    ]
    loads[1].wait()
    loads[2].wait()
    pl.semaphore_wait(barrier, 53)
    for copy in halo:
        copy.start()

    me = zh * 2 + c
    first = []
    for j in FAR_FIRST:
        peer, back = (me + j) % SIDE, (me + SIDE - j) % SIDE
        out = send(evp.at[peer], r1.at[me], sem_1s.at[j], sem_1r.at[j], *on_zc(peer))
        out.start()
        first.append((out, send(evp.at[peer], r1.at[back], sem_1s.at[j], sem_1r.at[j], *on_zc(back))))
    r1[pl.ds(me, 1)] = evp[pl.ds(me, 1)]

    for load in loads[3:]:
        load.wait()

    def place_slots(index, lon_out, hot_out):
        lon = (index * 10923) >> 22
        lat = index - lon * LAT
        lon_out[...] = jnp.broadcast_to(lon, (LEV, SLOTS))
        for n in range(SLOTS // CHUNK):
            rows = lax.broadcasted_iota(jnp.int32, (LAT, CHUNK), 0)
            hot = jnp.where(rows == lat[:, n * CHUNK : (n + 1) * CHUNK], 1.0, 0.0)
            hot_out[:, pl.ds(n * CHUNK, CHUNK)] = hot.astype(BF16)

    live = lax.broadcasted_iota(jnp.int32, (1, SLOTS), 1) < oc[0, 0]
    o0 = jnp.where(live, obs[0], 0.0)
    s1 = o0 / obs[1]
    obs[0] = o0
    obs[2] = s1
    terms[...] = wv[...] * s1
    gsend = [
        send(terms, terms_n, sem_gs.at[0], sem_gr.at[0], before, t),
        send(oiv, oiv_n, sem_gs.at[1], sem_gr.at[1], before, t),
    ]
    for copy in gsend:
        copy.start()
    place_slots(oiv[...], lonb, onehot)

    def pieces(x):
        high = x.astype(BF16)
        return high, (x - high.astype(F32)).astype(BF16)

    def spread(values, lons, hot):
        total = jnp.zeros((LON * LEV, LAT), F32)
        for n in range(SLOTS // CHUNK):
            cols = pl.ds(n * CHUNK, CHUNK)
            ids = lax.broadcasted_iota(jnp.int32, (LON, LEV, CHUNK), 0)
            placed = jnp.where(ids == lons[:, cols][None], values[:, cols][None], 0.0).reshape(LON * LEV, CHUNK)
            for piece in pieces(placed):
                total += lax.dot_general(piece, hot[:, cols], (((1,), (1,)), ((), ())), preferred_element_type=F32)
        return total.reshape(LON, LEV, LAT)

    def observe(field, row):
        high, low = pieces(field.reshape(LON * LEV, LAT))
        for n in range(SLOTS // CHUNK):
            cols = pl.ds(n * CHUNK, CHUNK)
            picked = jnp.dot(high, onehot[:, cols], preferred_element_type=F32)
            picked += jnp.dot(low, onehot[:, cols], preferred_element_type=F32)
            picked = picked.reshape(LON, LEV, CHUNK)
            here = lonb[:, cols]
            column = jnp.zeros((LEV, CHUNK), F32)
            for i in range(LON):
                column = jnp.where(here == i, picked[i], column)
            total = jnp.sum(column * wv[:, cols], axis=0, keepdims=True)
            slot = lax.broadcasted_iota(jnp.int32, (1, CHUNK), 1) + n * CHUNK
            obs[row, :, cols] = jnp.where(slot < oc[0, 0], total, 0.0)

    gb[...] = spread(terms, lonb, onehot)
    for lt in range(LAT // 128):
        sl = pl.ds(lt * 128, 128)
        u = gb[:, :, sl]
        for n, off in ((8, 0), (4, 8), (2, 12), (1, 14)):
            pair = u.reshape(n, 2, LEV, 128)
            hb[pl.ds(off, n), :, sl] = pair[:, 0] - pair[:, 1]
            u = pair[:, 0] + pair[:, 1]
        cu[pl.ds(place, 1), :, sl] = u
    coarse = []
    for j in range(1, 4):
        peer, back = (place + j) % 4, (place + 4 - j) % 4
        out = send(cu.at[place], cu.at[place], sem_cs.at[j], sem_cr.at[j], k, base + peer)
        out.start()
        coarse.append((out, send(cu.at[place], cu.at[back], sem_cs.at[j], sem_cr.at[j], k, base + back)))

    level_ids = lax.broadcasted_iota(jnp.int32, (LEV, LEV), 0)
    other_ids = lax.broadcasted_iota(jnp.int32, (LEV, LEV), 1)
    mixing = vmv[0] + jnp.where(level_ids == other_ids, 0.7, 0.0).astype(F32)
    for r in range(LEV):
        chosen = jnp.where(other_ids == (level_ids + r) % LEV, mixing, 0.0)
        mixf[r] = jnp.broadcast_to(jnp.sum(chosen, axis=1, keepdims=True), (LEV, LAT))
    mixb[0] = mixf[0]
    for r in range(1, LEV):
        mixb[r] = pltpu.roll(mixf[LEV - r], LEV - r, 0)
    lanes = lax.broadcasted_iota(jnp.int32, (LEV, LAT), 1)
    dn = jnp.where(lanes < LAT - 1, dfv[0], 0.0)
    dp = pltpu.roll(dn, 1, 1)
    latc[0] = dn
    latc[1] = dp
    latc[2] = 1.0 - dn - dp

    def weigh(start, count):
        cols = pl.ds(start, count)
        c = ac[1, cols]
        sq = c * c
        wts[0, cols] = (sq + c) * 0.5
        wts[1, cols] = 1.0 - sq
        wts[2, cols] = (sq - c) * 0.5

    for n in range(4):
        weigh(HALO + 4 * n, 4)

    def latitude(a):
        return latc[2] * a + latc[0] * pltpu.roll(a, LAT - 1, 2) + latc[1] * pltpu.roll(a, 1, 2)

    def couple(b, mix):
        total = mix[0] * b
        for r in range(1, LEV):
            total += mix[r] * pltpu.roll(b, LEV - r, 1)
        return total

    def forward(start, out):
        path = [(start, bufa, 0), (bufa, bufb, 0), (bufb, bufa, 0), (bufa, out, HALO)]
        for step, ((src, dst, off), blocks) in enumerate(zip(path, (6, 5, 5, 4))):

            def block(n, carry):
                i = step + 1 + 4 * n
                u = src[pl.ds(i - 1, 6)]
                a = wts[0, pl.ds(i, 4)] * u[0:4] + wts[1, pl.ds(i, 4)] * u[1:5] + wts[2, pl.ds(i, 4)] * u[2:6]
                dst[pl.ds(i - off, 4)] = couple(latitude(a), mixf)
                return carry

            lax.fori_loop(0, blocks, block, 0, unroll=True)

    def backward(start, out):
        path = [(start, bufa, 0), (bufa, bufb, 0), (bufb, bufa, 0), (bufa, out, HALO)]
        for step, ((src, dst, off), wide, narrow) in enumerate(zip(path, (6, 6, 5, 5), (6, 5, 5, 4))):

            def inner(n, carry):
                i = step + 4 * n
                bufg[pl.ds(i, 4)] = latitude(couple(src[pl.ds(i, 4)], mixb))
                return carry

            def outer(n, carry):
                i = step + 1 + 4 * n
                z = wts[1, pl.ds(i, 4)] * bufg[pl.ds(i, 4)]
                z += wts[0, pl.ds(i + 1, 4)] * bufg[pl.ds(i + 1, 4)]
                z += wts[2, pl.ds(i - 1, 4)] * bufg[pl.ds(i - 1, 4)]
                dst[pl.ds(i - off, 4)] = z
                return carry

            lax.fori_loop(0, wide, inner, 0, unroll=True)
            lax.fori_loop(0, narrow, outer, 0, unroll=True)

    for copy in halo:
        copy.wait()
    weigh(0, HALO)
    weigh(HALO + LON, HALO)
    forward(ac.at[0], mo.at[0])
    shift = send(mo.at[0], ma, sem_ts.at[0], sem_tr.at[0], later, t)
    asend = send(ac.at[0, pl.ds(HALO, LON)], an, sem_ts.at[1], sem_tr.at[1], before, t)
    shift.start()

    for out, came in first:
        came.wait_recv()
    turned = jnp.transpose(r1[...].reshape(LAT, 128))
    s2[...] = turned.reshape(SIDE, LON, LAT)
    second = []
    for j in FAR_FIRST:
        peer, back = (y + j) % SIDE, (y + SIDE - j) % SIDE
        out = send(s2.at[peer], r2.at[y], sem_2s.at[j], sem_2r.at[j], *on_y(peer))
        out.start()
        second.append((out, send(s2.at[peer], r2.at[back], sem_2s.at[j], sem_2r.at[j], *on_y(back))))
    r2[pl.ds(y, 1)] = s2[pl.ds(y, 1)]

    observe(ac[0, pl.ds(HALO, LON)], 3)
    q1 = obs[0] + obs[3]
    obs[3] = q1
    obs[4] = q1 / obs[1]

    htq[...] = spread(wv[...] * obs[4], lonb, onehot)

    for copy in gsend:
        copy.wait()
    place_slots(oiv_n[...], lonb_n, onehot_n)
    gx[pl.ds(HALO, LON)] = spread(terms_n, lonb_n, onehot_n)
    gedge = [
        send(gx.at[pl.ds(HALO, HALO)], gx.at[pl.ds(HALO + LON, HALO)], sem_hs.at[4], sem_hr.at[4], k, west),
        send(gx.at[pl.ds(LON, HALO)], gx.at[pl.ds(0, HALO)], sem_hs.at[5], sem_hr.at[5], k, east),
    ]
    for copy in gedge:
        copy.start()

    for out, came in coarse:
        came.wait_recv()
    for out, came in second:
        came.wait_recv()
    lane = lax.broadcasted_iota(jnp.int32, (LON, LAT), 1)
    for zz in range(4):
        for half in range(2):
            level = None
            for m in range(4):
                offset = (96 * (m - zz)) % LAT
                part = r2[half * 4 + m]
                moved = pltpu.roll(part, offset, 1) if offset else part
                level = moved if level is None else jnp.where(lane >= 96 * m, moved, level)
            vt[zz * 2 + half] = level
    vb[...] = jnp.swapaxes(vt[...], 0, 1)
    u = [cu[j] for j in range(4)]
    left, right = jnp.where(place < 2, u[0], u[2]), jnp.where(place < 2, u[1], u[3])
    total = (u[0] + u[1]) + jnp.where(place == 0, u[2] + u[3], -(u[2] + u[3]))
    coefficient = jnp.where(place % 2 == 0, total * (1 / 64), (left - right) * (1 / 32))
    wq[place] = coefficient * vb[0]
    wsend = []
    for j in range(1, 4):
        peer, back = (place + j) % 4, (place + 4 - j) % 4
        out = send(wq.at[place], wq.at[place], sem_ws.at[j], sem_wr.at[j], k, base + peer)
        out.start()
        wsend.append((out, send(wq.at[place], wq.at[back], sem_ws.at[j], sem_wr.at[j], k, base + back)))
    wside = [
        send(wq.at[place], wn.at[place], sem_ws.at[4], sem_wr.at[4 + place], k, (base + TILES - 1) % TILES),
        send(wq.at[place], wn.at[place], sem_ws.at[5], sem_wr.at[4 + place], k, (base + 4) % TILES),
    ]
    for copy in wside:
        copy.start()

    shift.wait()
    asend.start()
    for lt in range(LAT // 128):
        sl = pl.ds(lt * 128, 128)
        u = None
        for n, off, half in ((1, 14, 1 / 16), (2, 12, 1 / 8), (4, 8, 1 / 4), (8, 0, 1 / 2)):
            width = LON // n
            var = vb[:, :, sl].reshape(n, width, LEV, 128)[:, width // 2]
            d = hb[pl.ds(off, n), :, sl] * var * half
            u = jnp.concatenate([d, -d]) if u is None else jnp.stack([u + d, u - d], axis=1).reshape(2 * n, LEV, 128)
        dx[pl.ds(HALO, LON), :, sl] = ac[0, pl.ds(HALO, LON), :, sl] - jnp.where(k > 0, ma[:, :, sl], 0.0) - u
    edge = [
        send(dx.at[pl.ds(HALO, HALO)], dx.at[pl.ds(HALO + LON, HALO)], sem_hs.at[2], sem_hr.at[2], k, west),
        send(dx.at[pl.ds(LON, HALO)], dx.at[pl.ds(0, HALO)], sem_hs.at[3], sem_hr.at[3], k, east),
    ]
    for copy in edge:
        copy.start()
    for copy in gedge:
        copy.wait()
    backward(gx, mtg)
    observe(dx[pl.ds(HALO, LON)], 5)

    def state_part(n, acc):
        cols = pl.ds(4 * n, 4)
        g = gb[cols]
        f = g - jnp.where(k < WINDOWS - 1, mtg[cols], 0.0) + htq[cols]
        return acc[0] + jnp.sum(g * g, axis=0), acc[1] + jnp.sum(g * f, axis=0), acc[2] + jnp.sum(f * f, axis=0)

    zero = jnp.zeros((LEV, LAT), F32)
    gg, gf, ff = lax.fori_loop(0, 4, state_part, (zero, zero, zero), unroll=True)
    asend.wait()
    for out, came in wsend:
        came.wait_recv()

    @pl.when((place == 0) | (place == 3))
    def _():
        for j in range(4):
            send(wq.at[j], wn.at[j], sem_ws.at[4], sem_wr.at[4 + j], k, beside + j).wait_recv()

    for copy in edge:
        copy.wait()

    def on_tile(w, at):
        pair = jnp.where(at < 2, w[0] + w[2], w[0] - w[2])
        fine = jnp.where(at < 2, w[1], w[3])
        return pair + jnp.where(at % 2 == 0, fine, -fine)

    up[0] = jnp.where(place > 0, on_tile(wq, place - 1), on_tile(wn, 3))
    up[1] = on_tile(wq, place)
    up[2] = jnp.where(place < 3, on_tile(wq, place + 1), on_tile(wn, 0))
    for n, start, count in ((0, 0, HALO), (1, HALO, LON), (2, HALO + LON, HALO)):
        dx[pl.ds(start, count)] = dx[pl.ds(start, count)] - up[n][None]
    dd[...] = dx[pl.ds(HALO, LON)]

    def fold(x):
        x = jnp.sum(x, axis=0, keepdims=True)
        return sum(x[:, n : n + 128] for n in range(0, x.shape[1], 128))

    o0, q1 = obs[0], obs[3]
    picked = sum(jnp.dot(piece, onehot[...], preferred_element_type=F32) for piece in pieces(up[1]))
    flat = jnp.sum(picked * wv[...], axis=0, keepdims=True)
    h = q1 + obs[5] - jnp.where(live, flat, 0.0)
    sums = [fold(o0 * q1), fold(gg) + fold(q1 * q1), fold(o0 * h), fold(gf) + fold(q1 * h), fold(ff) + fold(h * h)]
    forward(dx, mo.at[1])

    def lam_part(n, acc):
        cols = pl.ds(4 * n, 4)
        a = an[cols]
        b = a - jnp.where(k < WINDOWS - 1, mo[0, cols], 0.0)
        e = b - jnp.where(k < WINDOWS - 1, mo[1, cols], 0.0)
        products = (a * b, b * b, a * e, b * e, e * e)
        return tuple(total + jnp.sum(product, axis=0) for total, product in zip(acc, products))

    acc = lax.fori_loop(0, 4, lam_part, (zero,) * 5, unroll=True)
    row = lax.broadcasted_iota(jnp.int32, (8, 128), 0)
    total = jnp.zeros((8, 128), F32)
    for n in range(5):
        total = jnp.where(row == n, sums[n] + fold(acc[n]), total)

    for stage, (me, ring, order, arr) in enumerate(((me_yc, on_yc, FAR_YC, arr1), (me_zx, on_zx, FAR_ZX, arr2))):
        count = len(order) + 1
        arr[0] = total
        for j in order:
            send(arr.at[0], arr.at[j], sem_a.at[stage, 0], sem_a.at[stage, 1], *ring((me + j) % count)).start()
        others = arr.at[pl.ds(1, count - 1)]
        send(others, others, sem_a.at[stage, 0], sem_a.at[stage, 1], *ring((me + 1) % count)).wait_recv()
        total = jnp.sum(arr[...], axis=0)
    total = jnp.sum(total, axis=1, keepdims=True)
    rq, qq, re, qe, ee = (total[n : n + 1] for n in range(5))
    alpha = rq / (qq + 1e-6)
    beta = alpha * (1e-6 - re + alpha * qe) / (qq - 2.0 * alpha * qe + alpha * alpha * ee + 1e-6)
    row = lax.broadcasted_iota(jnp.int32, (8, 128), 0)
    al[...] = jnp.where(row == 0, alpha, beta)
    ao[...] = ac[0, pl.ds(HALO, LON)]
    so[0] = obs[2]
    so[1] = obs[4]

    for out, came in first + second + coarse + wsend:
        out.wait_send()
    for copy in wside:
        copy.wait_send()
    for stage, (ring, arr) in enumerate(((on_yc, arr1), (on_zx, arr2))):
        others = arr.at[pl.ds(1, arr.shape[0] - 1)]
        send(others, others, sem_a.at[stage, 0], sem_a.at[stage, 1], *ring(0)).wait_send()


def finish(gb, dd, ao, so, al, mult, omult, incr):
    alpha, beta = al[0:1, 0:1], al[1:2, 0:1]
    both, cross = alpha + beta, alpha * beta
    wide_both, wide_cross = jnp.broadcast_to(both, (LEV, LAT)), jnp.broadcast_to(cross, (LEV, LAT))
    mult[0] = -wide_cross * gb[...]
    incr[0] = wide_both * ao[...] - wide_cross * dd[...]
    omult[...] = both * so[0] - cross * so[1]


def field(*lead):
    return pltpu.VMEM((*lead, LEV, LAT), F32)


SCRATCH = [
    field(2, WIDE),
    field(3, WIDE),
    pltpu.VMEM((LAT, SLOTS), BF16),
    pltpu.VMEM((LAT, SLOTS), BF16),
    pltpu.VMEM((LEV, SLOTS), jnp.int32),
    pltpu.VMEM((LEV, SLOTS), jnp.int32),
    pltpu.VMEM((6, 1, SLOTS), F32),
    pltpu.VMEM((1, SLOTS), jnp.int32),
    pltpu.VMEM((1, SLOTS), jnp.int32),
    pltpu.VMEM((LEV, SLOTS), F32),
    pltpu.VMEM((LEV, SLOTS), F32),
    pltpu.VMEM((LEV, SLOTS), F32),
    field(1),
    pltpu.VMEM((1, LEV, LEV), F32),
    field(3),
    field(LEV),
    field(LEV),
    field(WIDE),
    field(WIDE),
    field(WIDE),
    field(WIDE),
    field(2, LON),
    field(LON),
    field(LON),
    field(LON),
    field(LON),
    field(WIDE),
    field(LON),
    field(4),
    pltpu.VMEM((LAT // SIDE, TILES * LON), F32),
    pltpu.VMEM((SIDE, LAT // SIDE, 128), F32),
    pltpu.VMEM((SIDE, LAT // SIDE, 128), F32),
    pltpu.VMEM((SIDE, LON, LAT), F32),
    pltpu.VMEM((SIDE, LON, LAT), F32),
    pltpu.VMEM((LEV, LON, LAT), F32),
    field(LON),
    field(4),
    field(4),
    field(3),
    pltpu.VMEM((16, 8, 128), F32),
    pltpu.VMEM((32, 8, 128), F32),
] + [
    pltpu.SemaphoreType.DMA(shape)
    for shape in (
        (9,), (6,), (6,), (8,), (8,), (8,), (8,), (8,), (8,), (4,), (4,), (2,), (2,), (2,), (2,), (2, 2),
    )
]


def body(md, od, ov, ow, oi, oc, cr, df, vm, ev):
    inputs = (md[0], od, ov, ow[0], oi, oc, cr[0], df, vm, jnp.swapaxes(ev[0], 0, 1))
    inputs = [x if x is oc else pltpu.with_memory_space_constraint(x, pltpu.HBM) for x in inputs]
    hbm = [pl.BlockSpec(memory_space=pltpu.HBM)]
    vmem = pl.BlockSpec(memory_space=pltpu.VMEM)
    plane = jax.ShapeDtypeStruct((LON, LEV, LAT), F32)
    parts = pl.pallas_call(
        kernel,
        out_shape=(plane, plane, plane, jax.ShapeDtypeStruct((2, 1, SLOTS), F32), jax.ShapeDtypeStruct((8, 128), F32)),
        in_specs=hbm * 5 + [pl.BlockSpec(memory_space=pltpu.SMEM)] + hbm * 4,
        out_specs=(vmem,) * 5,
        scratch_shapes=SCRATCH,
        compiler_params=pltpu.CompilerParams(
            collective_id=0, has_side_effects=True, vmem_limit_bytes=40 * 1024 * 1024
        ),
        name="saddle",
    )(*inputs)
    return pl.pallas_call(
        finish,
        out_shape=(
            jax.ShapeDtypeStruct((1, LON, LEV, LAT), F32),
            jax.ShapeDtypeStruct((1, SLOTS), F32),
            jax.ShapeDtypeStruct((1, LON, LEV, LAT), F32),
        ),
        compiler_params=pltpu.CompilerParams(vmem_limit_bytes=8 * 1024 * 1024),
        name="finish",
    )(*parts)


def solution(mesh):
    in_specs = (
        P("tm", "space", None, None),
        P("tm", "space"),
        P("tm", "space"),
        P("tm", None, "space"),
        P("tm", "space"),
        P("tm", "space"),
        P("tm", "space", None, None),
        P("tm", None, None),
        P("tm", None, None),
        P("tm", None, "space"),
    )
    out_specs = (P("tm", "space", None, None), P("tm", "space"), P("tm", "space", None, None))
    return jax.shard_map(body, mesh=mesh, in_specs=in_specs, out_specs=out_specs, check_vma=False)
```

time: 58 us -> 53.2 us (0.917)
  local copies, waits for them, and re-layouts: 2.94 us -> 0 us
  Pallas kernels: 53.6 us -> 51.8 us
    unnamed x7 -> x0, local copies, waits for them, and re-layouts: 2.94 us -> none
    pallas_call x1 -> x2, Pallas kernels: 53.6 us -> 51.8 us  [the longest x1 51 us: body(): pl.pallas_call(kernel, out_shape=(plane, plane, plane, jax.ShapeDtypeStru...]
where the time goes in v3:
time: 53.2 us; the launch traced here: 53 us
  Pallas kernels  51.8 us (97%)
  between operations  1.29 us (2%)
    pallas_call x1, Pallas kernels, body(): pl.pallas_call(kernel, out_shape=(plane, plane, plane, jax.ShapeDtypeStru...  51 us

profile of v3, /device:TPU:1, one launch (start us, length us, event | category | flops | bytes accessed | tf_op | source)
XLA Modules:
  0.0 53.0 jit_solution(16474309234487432406)
XLA Ops:
  1.3 51.0 %saddle.1 = (f32[16,8,384]{2,1,0:T(8,128)S(1)}, f32[16,8,384]{2,1,0:T(8,128)S(1)}, f32[16,8,384]{2,1,0:T(8,128)S(1)}, f32[2,1,2048]{2,1,0:T(1,128)S(1)}, f32[8,128]{1,0:T(8,128)S(1)}) custom-call(f32[16,8,384]{2,1,0:T(8,128)} %bitcast.6, f32[1,2048]{1,0:T(1,128)} %od.1, f32[1,2048]{1,0:T(1,128)} %ov.1, f32[8,2048]{1,0:T(8,128)} %bitcast.9, s32[1,2048]{1,0:T(1,128)} %oi.1, ...), custom_call_target="tpu_custom_call" | custom-call | tf_op jit(solution)/shard_map/saddle/pallas_call | solution.py:516
  52.3 0.8 %finish.1 = (f32[1,16,8,384]{3,2,1,0:T(8,128)}, f32[1,2048]{1,0:T(1,128)}, f32[1,16,8,384]{3,2,1,0:T(8,128)}) custom-call(f32[16,8,384]{2,1,0:T(8,128)S(1)} %get-tuple-element.8.gb, f32[16,8,384]{2,1,0:T(8,128)S(1)} %get-tuple-element.9.dd, f32[16,8,384]{2,1,0:T(8,128)S(1)} %get-tuple-element.10.ao, f32[2,1,2048]{2,1,0:T(1,128)S(1)} %get-tuple-element.11.so, ...), custom_call_target="tpu_custom_call" | custom-call | tf_op jit(solution)/shard_map/finish/pallas_call | solution.py:527

commit v4 on v3

--- a/solution.py
+++ b/solution.py
@@ -24,7 +24,7 @@
     ac, wts, onehot, onehot_n, lonb, lonb_n, obs, oiv, oiv_n, wv, terms, terms_n, dfv, vmv, latc, mixf, mixb,
     gx, bufa, bufb, bufg, mo, ma, an, mtg, htq, dx,
     hb, cu, evv, evp, r1, s2, r2, vt, vb, wq, wn, up, arr1, arr2,
-    sem_load, sem_hs, sem_hr, sem_1s, sem_1r, sem_2s, sem_2r, sem_ws, sem_wr, sem_cs, sem_cr, sem_gs, sem_gr, sem_ts, sem_tr, sem_a,
+    sem_load, sem_hs, sem_hr, sem_1s, sem_1r, sem_2s, sem_2r, sem_ws, sem_wr, sem_cs, sem_cr, sem_gs, sem_gr, sem_ts, sem_tr, sem_a, sem_in,
 ):
     k = lax.axis_index("tm")
     t = lax.axis_index("space")
@@ -80,12 +80,15 @@
         pl.semaphore_signal(barrier, inc=1, device_id=(kk, tt), device_id_type=MESH)
 
     me_yc, me_zx = y * 2 + c, (zh * 2 + zl) * 4 + x
-    for j in FAR_ZX:
-        greet(*on_zx((me_zx + j) % 32))
     for j in FAR_YC:
         greet(*on_yc((me_yc + j) % 16))
+    for j in FAR_FIRST:
+        greet(*on_zx((me_zx + 4 * j) % 32))
     for j in range(1, 4):
         greet(k, tile_at((zh + j) % 4, y, 1 - c))
+        greet((x + j) % 4 * 2 + zl, t)
+    greet(later, t)
+    greet(before, t)
     greet(k, east)
     greet(k, west)
     beside = jnp.where(place == 0, base + TILES - 4, base + 4) % TILES
@@ -113,7 +116,7 @@
     ]
     loads[1].wait()
     loads[2].wait()
-    pl.semaphore_wait(barrier, 53)
+    pl.semaphore_wait(barrier, 34)
     for copy in halo:
         copy.start()
 
@@ -125,6 +128,10 @@
         out.start()
         first.append((out, send(evp.at[peer], r1.at[back], sem_1s.at[j], sem_1r.at[j], *on_zc(back))))
     r1[pl.ds(me, 1)] = evp[pl.ds(me, 1)]
+
+    for j in FAR_FIRST:
+        kk, tt = on_zx((me_zx + 4 * j) % 32)
+        pl.semaphore_signal(sem_in, inc=1, device_id=(kk, tt), device_id_type=MESH)
 
     for load in loads[3:]:
         load.wait()
@@ -274,6 +281,7 @@
     shift = send(mo.at[0], ma, sem_ts.at[0], sem_tr.at[0], later, t)
     asend = send(ac.at[0, pl.ds(HALO, LON)], an, sem_ts.at[1], sem_tr.at[1], before, t)
     shift.start()
+    asend.start()
 
     for out, came in first:
         came.wait_recv()
@@ -339,7 +347,6 @@
         copy.start()
 
     shift.wait()
-    asend.start()
     for lt in range(LAT // 128):
         sl = pl.ds(lt * 128, 128)
         u = None
@@ -368,7 +375,6 @@
 
     zero = jnp.zeros((LEV, LAT), F32)
     gg, gf, ff = lax.fori_loop(0, 4, state_part, (zero, zero, zero), unroll=True)
-    asend.wait()
     for out, came in wsend:
         came.wait_recv()
 
@@ -402,6 +408,8 @@
     h = q1 + obs[5] - jnp.where(live, flat, 0.0)
     sums = [fold(o0 * q1), fold(gg) + fold(q1 * q1), fold(o0 * h), fold(gf) + fold(q1 * h), fold(ff) + fold(h * h)]
     forward(dx, mo.at[1])
+
+    asend.wait()
 
     def lam_part(n, acc):
         cols = pl.ds(4 * n, 4)
@@ -419,6 +427,8 @@
 
     for stage, (me, ring, order, arr) in enumerate(((me_yc, on_yc, FAR_YC, arr1), (me_zx, on_zx, FAR_ZX, arr2))):
         count = len(order) + 1
+        if stage == 1:
+            pl.semaphore_wait(sem_in, SIDE - 1)
         arr[0] = total
         for j in order:
             send(arr.at[0], arr.at[j], sem_a.at[stage, 0], sem_a.at[stage, 1], *ring((me + j) % count)).start()
@@ -504,7 +514,7 @@
     for shape in (
         (9,), (6,), (6,), (8,), (8,), (8,), (8,), (8,), (8,), (4,), (4,), (2,), (2,), (2,), (2,), (2, 2),
     )
-]
+] + [pltpu.SemaphoreType.REGULAR]
 
 
 def body(md, od, ov, ow, oi, oc, cr, df, vm, ev):

time: 53.2 us -> 50.5 us (0.949)
  Pallas kernels: 51.8 us -> 49.1 us
    pallas_call x1, Pallas kernels: 51 us -> 48.3 us  [body(): pl.pallas_call(kernel, out_shape=(plane, plane, plane, jax.ShapeDtypeStru...]
where the time goes in v4:
time: 50.5 us; the launch traced here: 50.4 us
  Pallas kernels  49.1 us (97%)
  between operations  1.29 us (3%)
    pallas_call x1, Pallas kernels, body(): pl.pallas_call(kernel, out_shape=(plane, plane, plane, jax.ShapeDtypeStru...  48.3 us

profile of v4, /device:TPU:1, one launch (start us, length us, event | category | flops | bytes accessed | tf_op | source)
XLA Modules:
  0.0 50.4 jit_solution(16636713362563448483)
XLA Ops:
  1.3 48.3 %saddle.1 = (f32[16,8,384]{2,1,0:T(8,128)S(1)}, f32[16,8,384]{2,1,0:T(8,128)S(1)}, f32[16,8,384]{2,1,0:T(8,128)S(1)}, f32[2,1,2048]{2,1,0:T(1,128)S(1)}, f32[8,128]{1,0:T(8,128)S(1)}) custom-call(f32[16,8,384]{2,1,0:T(8,128)} %bitcast.6, f32[1,2048]{1,0:T(1,128)} %od.1, f32[1,2048]{1,0:T(1,128)} %ov.1, f32[8,2048]{1,0:T(8,128)} %bitcast.9, s32[1,2048]{1,0:T(1,128)} %oi.1, ...), custom_call_target="tpu_custom_call" | custom-call | tf_op jit(solution)/shard_map/saddle/pallas_call | solution.py:526
  49.6 0.8 %finish.1 = (f32[1,16,8,384]{3,2,1,0:T(8,128)}, f32[1,2048]{1,0:T(1,128)}, f32[1,16,8,384]{3,2,1,0:T(8,128)}) custom-call(f32[16,8,384]{2,1,0:T(8,128)S(1)} %get-tuple-element.8.gb, f32[16,8,384]{2,1,0:T(8,128)S(1)} %get-tuple-element.9.dd, f32[16,8,384]{2,1,0:T(8,128)S(1)} %get-tuple-element.10.ao, f32[2,1,2048]{2,1,0:T(1,128)S(1)} %get-tuple-element.11.so, ...), custom_call_target="tpu_custom_call" | custom-call | tf_op jit(solution)/shard_map/finish/pallas_call | solution.py:537

commit v5 on v4

--- a/solution.py
+++ b/solution.py
@@ -54,6 +54,31 @@
 
     def on_zx(place):
         return place % 4 * 2 + place // 4 % 2, tile_at(place // 8, y, c)
+
+    barrier = pltpu.get_barrier_semaphore()
+
+    def greet(kk, tt):
+        pl.semaphore_signal(barrier, inc=1, device_id=(kk, tt), device_id_type=MESH)
+
+    me_yc, me_zx = y * 2 + c, (zh * 2 + zl) * 4 + x
+    for j in FAR_YC:
+        greet(*on_yc((me_yc + j) % 16))
+    for j in FAR_FIRST:
+        greet(*on_zx((me_zx + 4 * j) % 32))
+    for j in range(1, 4):
+        greet(k, tile_at((zh + j) % 4, y, 1 - c))
+        greet((x + j) % 4 * 2 + zl, t)
+    greet(later, t)
+    greet(before, t)
+    greet(k, east)
+    greet(k, west)
+    beside = jnp.where(place == 0, base + TILES - 4, base + 4) % TILES
+
+    @pl.when((place == 0) | (place == 3))
+    def _():
+        for j in range(4):
+            greet(k, beside + j)
+
 
     loads = [
         pltpu.make_async_copy(src, dst, sem_load.at[n])
@@ -74,31 +99,6 @@
     for load in loads:
         load.start()
 
-    barrier = pltpu.get_barrier_semaphore()
-
-    def greet(kk, tt):
-        pl.semaphore_signal(barrier, inc=1, device_id=(kk, tt), device_id_type=MESH)
-
-    me_yc, me_zx = y * 2 + c, (zh * 2 + zl) * 4 + x
-    for j in FAR_YC:
-        greet(*on_yc((me_yc + j) % 16))
-    for j in FAR_FIRST:
-        greet(*on_zx((me_zx + 4 * j) % 32))
-    for j in range(1, 4):
-        greet(k, tile_at((zh + j) % 4, y, 1 - c))
-        greet((x + j) % 4 * 2 + zl, t)
-    greet(later, t)
-    greet(before, t)
-    greet(k, east)
-    greet(k, west)
-    beside = jnp.where(place == 0, base + TILES - 4, base + 4) % TILES
-
-    @pl.when((place == 0) | (place == 3))
-    def _():
-        for j in range(4):
-            greet(k, beside + j)
-
-
     lane_v = lax.broadcasted_iota(jnp.int32, (LAT // SIDE, 128), 1)
     loads[0].wait()
     for zz in range(4):
@@ -110,29 +110,6 @@
                 moved = pltpu.roll(source, offset, 1) if offset else source
                 block = moved if block is None else jnp.where(lane_v >= yy * 16, moved, block)
             evp[zz * 2 + cc] = block
-    halo = [
-        send(ac.at[:, pl.ds(HALO, HALO)], ac.at[:, pl.ds(HALO + LON, HALO)], sem_hs.at[0], sem_hr.at[0], k, west),
-        send(ac.at[:, pl.ds(LON, HALO)], ac.at[:, pl.ds(0, HALO)], sem_hs.at[1], sem_hr.at[1], k, east),
-    ]
-    loads[1].wait()
-    loads[2].wait()
-    pl.semaphore_wait(barrier, 34)
-    for copy in halo:
-        copy.start()
-
-    me = zh * 2 + c
-    first = []
-    for j in FAR_FIRST:
-        peer, back = (me + j) % SIDE, (me + SIDE - j) % SIDE
-        out = send(evp.at[peer], r1.at[me], sem_1s.at[j], sem_1r.at[j], *on_zc(peer))
-        out.start()
-        first.append((out, send(evp.at[peer], r1.at[back], sem_1s.at[j], sem_1r.at[j], *on_zc(back))))
-    r1[pl.ds(me, 1)] = evp[pl.ds(me, 1)]
-
-    for j in FAR_FIRST:
-        kk, tt = on_zx((me_zx + 4 * j) % 32)
-        pl.semaphore_signal(sem_in, inc=1, device_id=(kk, tt), device_id_type=MESH)
-
     for load in loads[3:]:
         load.wait()
 
@@ -151,12 +128,6 @@
     obs[0] = o0
     obs[2] = s1
     terms[...] = wv[...] * s1
-    gsend = [
-        send(terms, terms_n, sem_gs.at[0], sem_gr.at[0], before, t),
-        send(oiv, oiv_n, sem_gs.at[1], sem_gr.at[1], before, t),
-    ]
-    for copy in gsend:
-        copy.start()
     place_slots(oiv[...], lonb, onehot)
 
     def pieces(x):
@@ -188,6 +159,33 @@
             slot = lax.broadcasted_iota(jnp.int32, (1, CHUNK), 1) + n * CHUNK
             obs[row, :, cols] = jnp.where(slot < oc[0, 0], total, 0.0)
 
+    halo = [
+        send(ac.at[:, pl.ds(HALO, HALO)], ac.at[:, pl.ds(HALO + LON, HALO)], sem_hs.at[0], sem_hr.at[0], k, west),
+        send(ac.at[:, pl.ds(LON, HALO)], ac.at[:, pl.ds(0, HALO)], sem_hs.at[1], sem_hr.at[1], k, east),
+    ]
+    loads[1].wait()
+    loads[2].wait()
+    pl.semaphore_wait(barrier, 34)
+
+    me = zh * 2 + c
+    first = []
+    for j in FAR_FIRST:
+        peer, back = (me + j) % SIDE, (me + SIDE - j) % SIDE
+        out = send(evp.at[peer], r1.at[me], sem_1s.at[j], sem_1r.at[j], *on_zc(peer))
+        out.start()
+        first.append((out, send(evp.at[peer], r1.at[back], sem_1s.at[j], sem_1r.at[j], *on_zc(back))))
+    r1[pl.ds(me, 1)] = evp[pl.ds(me, 1)]
+
+    for copy in halo:
+        copy.start()
+
+    gsend = [
+        send(terms, terms_n, sem_gs.at[0], sem_gr.at[0], before, t),
+        send(oiv, oiv_n, sem_gs.at[1], sem_gr.at[1], before, t),
+    ]
+    for copy in gsend:
+        copy.start()
+
     gb[...] = spread(terms, lonb, onehot)
     for lt in range(LAT // 128):
         sl = pl.ds(lt * 128, 128)
@@ -197,6 +195,10 @@
             hb[pl.ds(off, n), :, sl] = pair[:, 0] - pair[:, 1]
             u = pair[:, 0] + pair[:, 1]
         cu[pl.ds(place, 1), :, sl] = u
+    for j in FAR_FIRST:
+        kk, tt = on_zx((me_zx + 4 * j) % 32)
+        pl.semaphore_signal(sem_in, inc=1, device_id=(kk, tt), device_id_type=MESH)
+
     coarse = []
     for j in range(1, 4):
         peer, back = (place + j) % 4, (place + 4 - j) % 4
@@ -283,6 +285,12 @@
     shift.start()
     asend.start()
 
+    observe(ac[0, pl.ds(HALO, LON)], 3)
+    q1 = obs[0] + obs[3]
+    obs[3] = q1
+    obs[4] = q1 / obs[1]
+
+
     for out, came in first:
         came.wait_recv()
     turned = jnp.transpose(r1[...].reshape(LAT, 128))
@@ -295,13 +303,6 @@
         second.append((out, send(s2.at[peer], r2.at[back], sem_2s.at[j], sem_2r.at[j], *on_y(back))))
     r2[pl.ds(y, 1)] = s2[pl.ds(y, 1)]
 
-    observe(ac[0, pl.ds(HALO, LON)], 3)
-    q1 = obs[0] + obs[3]
-    obs[3] = q1
-    obs[4] = q1 / obs[1]
-
-    htq[...] = spread(wv[...] * obs[4], lonb, onehot)
-
     for copy in gsend:
         copy.wait()
     place_slots(oiv_n[...], lonb_n, onehot_n)
@@ -312,6 +313,8 @@
     ]
     for copy in gedge:
         copy.start()
+
+    htq[...] = spread(wv[...] * obs[4], lonb, onehot)
 
     for out, came in coarse:
         came.wait_recv()
@@ -424,6 +427,9 @@
     total = jnp.zeros((8, 128), F32)
     for n in range(5):
         total = jnp.where(row == n, sums[n] + fold(acc[n]), total)
+    diagonal = row == lax.broadcasted_iota(jnp.int32, (8, 128), 1)
+    total = jnp.sum(total, axis=1, keepdims=True)
+    total = jnp.sum(jnp.where(diagonal, total, 0.0), axis=0, keepdims=True)
 
     for stage, (me, ring, order, arr) in enumerate(((me_yc, on_yc, FAR_YC, arr1), (me_zx, on_zx, FAR_ZX, arr2))):
         count = len(order) + 1
@@ -435,7 +441,7 @@
         others = arr.at[pl.ds(1, count - 1)]
         send(others, others, sem_a.at[stage, 0], sem_a.at[stage, 1], *ring((me + 1) % count)).wait_recv()
         total = jnp.sum(arr[...], axis=0)
-    total = jnp.sum(total, axis=1, keepdims=True)
+    total = jnp.sum(jnp.where(diagonal, total, 0.0), axis=1, keepdims=True)
     rq, qq, re, qe, ee = (total[n : n + 1] for n in range(5))
     alpha = rq / (qq + 1e-6)
     beta = alpha * (1e-6 - re + alpha * qe) / (qq - 2.0 * alpha * qe + alpha * alpha * ee + 1e-6)
@@ -507,8 +513,8 @@
     field(4),
     field(4),
     field(3),
-    pltpu.VMEM((16, 8, 128), F32),
-    pltpu.VMEM((32, 8, 128), F32),
+    pltpu.VMEM((16, 1, 128), F32),
+    pltpu.VMEM((32, 1, 128), F32),
 ] + [
     pltpu.SemaphoreType.DMA(shape)
     for shape in (

time: 50.5 us -> 48.2 us (0.954)
  Pallas kernels: 49.1 us -> 46.7 us
    pallas_call x1, Pallas kernels: 48.3 us -> 45.9 us  [body(): pl.pallas_call(kernel, out_shape=(plane, plane, plane, jax.ShapeDtypeStru...]
where the time goes in v5:
time: 48.2 us; the launch traced here: 48 us
  Pallas kernels  46.7 us (97%)
  between operations  1.29 us (3%)
    pallas_call x1, Pallas kernels, body(): pl.pallas_call(kernel, out_shape=(plane, plane, plane, jax.ShapeDtypeStru...  45.9 us

profile of v5, /device:TPU:1, one launch (start us, length us, event | category | flops | bytes accessed | tf_op | source)
XLA Modules:
  0.0 48.0 jit_solution(6652749652785989933)
XLA Ops:
  1.3 45.9 %saddle.1 = (f32[16,8,384]{2,1,0:T(8,128)S(1)}, f32[16,8,384]{2,1,0:T(8,128)S(1)}, f32[16,8,384]{2,1,0:T(8,128)S(1)}, f32[2,1,2048]{2,1,0:T(1,128)S(1)}, f32[8,128]{1,0:T(8,128)S(1)}) custom-call(f32[16,8,384]{2,1,0:T(8,128)} %bitcast.6, f32[1,2048]{1,0:T(1,128)} %od.1, f32[1,2048]{1,0:T(1,128)} %ov.1, f32[8,2048]{1,0:T(8,128)} %bitcast.9, s32[1,2048]{1,0:T(1,128)} %oi.1, ...), custom_call_target="tpu_custom_call" | custom-call | tf_op jit(solution)/shard_map/saddle/pallas_call | solution.py:532
  47.2 0.8 %finish.1 = (f32[1,16,8,384]{3,2,1,0:T(8,128)}, f32[1,2048]{1,0:T(1,128)}, f32[1,16,8,384]{3,2,1,0:T(8,128)}) custom-call(f32[16,8,384]{2,1,0:T(8,128)S(1)} %get-tuple-element.8.gb, f32[16,8,384]{2,1,0:T(8,128)S(1)} %get-tuple-element.9.dd, f32[16,8,384]{2,1,0:T(8,128)S(1)} %get-tuple-element.10.ao, f32[2,1,2048]{2,1,0:T(1,128)S(1)} %get-tuple-element.11.so, ...), custom_call_target="tpu_custom_call" | custom-call | tf_op jit(solution)/shard_map/finish/pallas_call | solution.py:543

commit v6 on v5

--- a/solution.py
+++ b/solution.py
@@ -254,6 +254,14 @@
                 return carry
 
             lax.fori_loop(0, blocks, block, 0, unroll=True)
+
+    def forward_in(start, out, parts):
+        path = [(start, bufa, 0), (bufa, bufb, 0), (bufb, bufa, 0), (bufa, out, HALO)]
+        for (src, dst, off), blocks in zip(path, parts):
+            for i, n in blocks:
+                u = src[pl.ds(i - 1, n + 2)]
+                a = wts[0, pl.ds(i, n)] * u[0:n] + wts[1, pl.ds(i, n)] * u[1 : n + 1] + wts[2, pl.ds(i, n)] * u[2 : n + 2]
+                dst[pl.ds(i - off, n)] = couple(latitude(a), mixf)
 
     def backward(start, out):
         path = [(start, bufa, 0), (bufa, bufb, 0), (bufb, bufa, 0), (bufa, out, HALO)]
@@ -349,6 +357,9 @@
     for copy in wside:
         copy.start()
 
+    ao[...] = ac[0, pl.ds(HALO, LON)]
+    so[0] = obs[2]
+    so[1] = obs[4]
     shift.wait()
     for lt in range(LAT // 128):
         sl = pl.ds(lt * 128, 128)
@@ -365,10 +376,10 @@
     ]
     for copy in edge:
         copy.start()
+    observe(dx[pl.ds(HALO, LON)], 5)
     for copy in gedge:
         copy.wait()
     backward(gx, mtg)
-    observe(dx[pl.ds(HALO, LON)], 5)
 
     def state_part(n, acc):
         cols = pl.ds(4 * n, 4)
@@ -381,24 +392,15 @@
     for out, came in wsend:
         came.wait_recv()
 
-    @pl.when((place == 0) | (place == 3))
-    def _():
-        for j in range(4):
-            send(wq.at[j], wn.at[j], sem_ws.at[4], sem_wr.at[4 + j], k, beside + j).wait_recv()
-
-    for copy in edge:
-        copy.wait()
-
     def on_tile(w, at):
         pair = jnp.where(at < 2, w[0] + w[2], w[0] - w[2])
         fine = jnp.where(at < 2, w[1], w[3])
         return pair + jnp.where(at % 2 == 0, fine, -fine)
 
-    up[0] = jnp.where(place > 0, on_tile(wq, place - 1), on_tile(wn, 3))
     up[1] = on_tile(wq, place)
-    up[2] = jnp.where(place < 3, on_tile(wq, place + 1), on_tile(wn, 0))
-    for n, start, count in ((0, 0, HALO), (1, HALO, LON), (2, HALO + LON, HALO)):
-        dx[pl.ds(start, count)] = dx[pl.ds(start, count)] - up[n][None]
+    for copy in edge:
+        copy.wait_send()
+    dx[pl.ds(HALO, LON)] = dx[pl.ds(HALO, LON)] - up[1][None]
     dd[...] = dx[pl.ds(HALO, LON)]
 
     def fold(x):
@@ -410,8 +412,21 @@
     flat = jnp.sum(picked * wv[...], axis=0, keepdims=True)
     h = q1 + obs[5] - jnp.where(live, flat, 0.0)
     sums = [fold(o0 * q1), fold(gg) + fold(q1 * q1), fold(o0 * h), fold(gf) + fold(q1 * h), fold(ff) + fold(h * h)]
-    forward(dx, mo.at[1])
-
+    inner = [[(i, min(4, 19 - step - i)) for i in range(5 + step, 19 - step, 4)] for step in range(4)]
+    forward_in(dx, mo.at[1], inner)
+    for copy in edge:
+        copy.wait_recv()
+
+    @pl.when((place == 0) | (place == 3))
+    def _():
+        for j in range(4):
+            send(wq.at[j], wn.at[j], sem_ws.at[4], sem_wr.at[4 + j], k, beside + j).wait_recv()
+
+    up[0] = jnp.where(place > 0, on_tile(wq, place - 1), on_tile(wn, 3))
+    up[2] = jnp.where(place < 3, on_tile(wq, place + 1), on_tile(wn, 0))
+    for n, start in ((0, 0), (2, HALO + LON)):
+        dx[pl.ds(start, HALO)] = dx[pl.ds(start, HALO)] - up[n][None]
+    forward_in(dx, mo.at[1], [[(1 + step, 4), (19 - step, 4)] for step in range(4)])
     asend.wait()
 
     def lam_part(n, acc):
@@ -447,9 +462,6 @@
     beta = alpha * (1e-6 - re + alpha * qe) / (qq - 2.0 * alpha * qe + alpha * alpha * ee + 1e-6)
     row = lax.broadcasted_iota(jnp.int32, (8, 128), 0)
     al[...] = jnp.where(row == 0, alpha, beta)
-    ao[...] = ac[0, pl.ds(HALO, LON)]
-    so[0] = obs[2]
-    so[1] = obs[4]
 
     for out, came in first + second + coarse + wsend:
         out.wait_send()

time: 48.2 us -> 47.7 us (0.990)
  Pallas kernels: 46.7 us -> 46.2 us
    pallas_call x1, Pallas kernels: 45.9 us -> 45.4 us  [body(): pl.pallas_call(kernel, out_shape=(plane, plane, plane, jax.ShapeDtypeStru...]
where the time goes in v6:
time: 47.7 us; the launch traced here: 47.5 us
  Pallas kernels  46.2 us (97%)
  between operations  1.29 us (3%)
    pallas_call x1, Pallas kernels, body(): pl.pallas_call(kernel, out_shape=(plane, plane, plane, jax.ShapeDtypeStru...  45.4 us

profile of v6, /device:TPU:1, one launch (start us, length us, event | category | flops | bytes accessed | tf_op | source)
XLA Modules:
  0.0 47.5 jit_solution(14506143377178244232)
XLA Ops:
  1.3 45.4 %saddle.1 = (f32[16,8,384]{2,1,0:T(8,128)S(1)}, f32[16,8,384]{2,1,0:T(8,128)S(1)}, f32[16,8,384]{2,1,0:T(8,128)S(1)}, f32[2,1,2048]{2,1,0:T(1,128)S(1)}, f32[8,128]{1,0:T(8,128)S(1)}) custom-call(f32[16,8,384]{2,1,0:T(8,128)} %bitcast.6, f32[1,2048]{1,0:T(1,128)} %od.1, f32[1,2048]{1,0:T(1,128)} %ov.1, f32[8,2048]{1,0:T(8,128)} %bitcast.9, s32[1,2048]{1,0:T(1,128)} %oi.1, ...), custom_call_target="tpu_custom_call" | custom-call | tf_op jit(solution)/shard_map/saddle/pallas_call | solution.py:544
  46.7 0.8 %finish.1 = (f32[1,16,8,384]{3,2,1,0:T(8,128)}, f32[1,2048]{1,0:T(1,128)}, f32[1,16,8,384]{3,2,1,0:T(8,128)}) custom-call(f32[16,8,384]{2,1,0:T(8,128)S(1)} %get-tuple-element.8.gb, f32[16,8,384]{2,1,0:T(8,128)S(1)} %get-tuple-element.9.dd, f32[16,8,384]{2,1,0:T(8,128)S(1)} %get-tuple-element.10.ao, f32[2,1,2048]{2,1,0:T(1,128)S(1)} %get-tuple-element.11.so, ...), custom_call_target="tpu_custom_call" | custom-call | tf_op jit(solution)/shard_map/finish/pallas_call | solution.py:555
